TPU v7x, 256 devices: a whole 4x4x8 slice. The times are simulated.
256 devices in a mesh: group: 8 (over z_hi, x), prompts: 32 (over z_lo, y, core).
Axes of the slice: x: 4, y: 4, z: 8 (z_hi: 2, z_lo: 4; z = z_hi * 4 + z_lo), core: 2. Of those that a mesh axis runs over, the one named last changes fastest.
Arguments:
- queries: bfloat16 [32, 8, 256, 4096], P('prompts', 'group'), may hold values from -6 to 6
- resp_kv: bfloat16 [32, 8, 256, 2, 512], P('prompts', 'group'), may hold values from -6 to 6
- prefix_kv: bfloat16 [32, 8, 256, 2, 512], P('prompts', 'group'), may hold values from -6 to 6
- norm_gains: float32 [2, 128], replicated, may hold values from 0.25 to 1.75
- dout: bfloat16 [32, 8, 256, 4096], P('prompts', 'group'), may hold values from -48 to 48
- lengths: int32 [32, 8], P('prompts', 'group'), may hold values from 1 to 256, as said below
- rewards: int32 [32, 8], P('prompts', 'group'), may hold values from 0 to 3
- owner: int32 [32], P('prompts'), may hold values from 0 to 7
Outputs:
- d_queries: bfloat16 [32, 8, 256, 4096], P('prompts', 'group')
- d_resp_kv: bfloat16 [32, 8, 256, 2, 512], P('prompts', 'group')
- d_prefix_kv: bfloat16 [32, 8, 256, 2, 512], P('prompts', 'group')
- d_gains: float32 [2, 128], replicated
Inputs may be any that keep to these rules, and one draw needn't show every extreme that they name: `lengths`: one response of the batch has exactly 256 live tokens.
All inputs are finite; a program needn't handle non-finite values.
Results may differ from a plain program's by a relative error of at most 0.012.
Values may be sent and summed in bfloat16 or wider, within the bound.
A program may use at most 64 MiB of HBM per device.

v0:
```python
from functools import partial

import jax
import jax.numpy as jnp
from jax import lax
from jax.sharding import PartitionSpec as P

HD = 128


EPSILON = 1e-06
THETA = 1000000.0


def broadcast(block, axis, holder):
    block = jnp.where(lax.axis_index(axis) == holder, block, jnp.zeros_like(block))
    return lax.psum(block, axis)


def rotate(values, cosine, sine_table):
    half_width = values.shape[-1] // 2
    lower_half = values[..., :half_width]
    upper_half = values[..., half_width:]
    return jnp.concatenate(
        [
            lower_half * cosine - upper_half * sine_table,
            upper_half * cosine + lower_half * sine_table,
        ],
        -1,
    )


def normalize(values, gain):
    return values * lax.rsqrt(jnp.mean(values * values, -1, keepdims=True) + EPSILON) * gain


def prepare(raw_queries, raw_keys, norm_gains, offset):
    tokens = raw_queries.shape[0]
    width = raw_queries.shape[-1]
    positions = offset + jnp.arange(tokens, dtype=jnp.float32)
    frequency = THETA ** (-2.0 * jnp.arange(width // 2, dtype=jnp.float32) / width)
    angles = positions[:, None] * frequency[None, :]
    cosine = jnp.cos(angles)[:, None, :]
    sine_table = jnp.sin(angles)[:, None, :]
    return (
        rotate(normalize(raw_queries, norm_gains[0]), cosine, sine_table),
        rotate(normalize(raw_keys, norm_gains[1]), cosine, sine_table),
    )


def head_grads(head_queries, head_keys, head_values, head_cot):
    tokens = head_queries.shape[0]
    key_count = head_keys.shape[0]
    prefix_rows = key_count - tokens
    score_scale = head_queries.shape[-1] ** (-0.5)
    scores = (
        jnp.einsum("tgd,sd->gts", head_queries, head_keys, preferred_element_type=jnp.float32)
        * score_scale
    )
    row_index = jnp.arange(tokens)[:, None]
    col_index = jnp.arange(key_count)[None, :]
    visible = (col_index < prefix_rows) | (col_index - prefix_rows <= row_index)
    exponents = jnp.where(visible[None], jnp.exp(scores), 0.0)
    weights = exponents / jnp.sum(exponents, -1, keepdims=True)
    weights_b = weights.astype(jnp.bfloat16)
    outputs = jnp.einsum("gts,sd->gtd", weights_b, head_values, preferred_element_type=jnp.float32)
    row_dots = jnp.einsum("tgd,gtd->gt", head_cot.astype(jnp.float32), outputs)
    prob_grad = jnp.einsum("tgd,sd->gts", head_cot, head_values, preferred_element_type=jnp.float32)
    score_grad = (weights * (prob_grad - row_dots[..., None])).astype(jnp.bfloat16)
    query_grad = (
        jnp.einsum("gts,sd->tgd", score_grad, head_keys, preferred_element_type=jnp.float32)
        * score_scale
    )
    key_grad = (
        jnp.einsum("gts,tgd->sd", score_grad, head_queries, preferred_element_type=jnp.float32)
        * score_scale
    )
    value_grad = jnp.einsum("gts,tgd->sd", weights_b, head_cot, preferred_element_type=jnp.float32)
    return (query_grad, key_grad, value_grad)


def body(queries, resp_kv, prefix_kv, norm_gains, dout, lengths, rewards, owner):
    group_size = lax.axis_size("group")
    my_index = lax.axis_index("group")
    owner_index = owner.reshape(())
    reward = rewards.reshape(()).astype(jnp.float32)
    reward_total, square_total = lax.psum((reward, reward * reward), "group")
    mean_reward = reward_total / group_size
    spread = jnp.sqrt(jnp.maximum(square_total / group_size - mean_reward * mean_reward, 0.0))
    advantage = (reward - mean_reward) / jnp.maximum(spread, 1.0)
    local_queries = queries[0, 0]
    local_kv = resp_kv[0, 0]
    local_dout = dout[0, 0]
    prefix_slot = prefix_kv[0, 0]
    length = lengths.reshape(())
    tokens = local_queries.shape[0]
    prefix_rows = prefix_slot.shape[0]
    query_heads = local_queries.shape[-1] // HD
    kv_heads = local_kv.shape[-1] // HD
    group_width = query_heads // kv_heads
    raw_queries = local_queries.astype(jnp.float32).reshape(tokens, query_heads, HD)
    raw_keys = local_kv[:, 0].astype(jnp.float32).reshape(tokens, kv_heads, HD)
    (rotated_q, rotated_k), backward = jax.vjp(
        partial(prepare, offset=prefix_rows), raw_queries, raw_keys, norm_gains
    )
    query_b = rotated_q.astype(jnp.bfloat16)
    key_b = rotated_k.astype(jnp.bfloat16)
    live_rows = jnp.arange(tokens) < length
    cotangent = jnp.where(live_rows[:, None], local_dout.astype(jnp.float32) * advantage, 0.0)
    cotangent = cotangent.astype(jnp.bfloat16).reshape(tokens, query_heads, HD)
    resp_values = local_kv[:, 1].reshape(tokens, kv_heads, HD)
    shared = broadcast(prefix_slot, "group", owner_index)
    query_parts = []
    key_parts = []
    value_parts = []
    prefix_parts = []
    for kv_head in range(kv_heads):
        first_head = kv_head * group_width
        column_start = kv_head * HD
        head_prefix = shared[:, :, column_start : column_start + HD]
        head_keys = jnp.concatenate([head_prefix[:, 0], key_b[:, kv_head]], 0)
        head_values = jnp.concatenate([head_prefix[:, 1], resp_values[:, kv_head]], 0)
        query_grad, key_grad, value_grad = head_grads(
            query_b[:, first_head : first_head + group_width],
            head_keys,
            head_values,
            cotangent[:, first_head : first_head + group_width],
        )
        prefix_grad = jnp.stack([key_grad[:prefix_rows], value_grad[:prefix_rows]], 1)
        prefix_parts.append(prefix_grad)
        query_parts.append(query_grad)
        key_parts.append(key_grad[prefix_rows:])
        value_parts.append(value_grad[prefix_rows:])
    prefix_total = jnp.concatenate(prefix_parts, -1)
    prefix_total = lax.psum(prefix_total, "group")
    query_grads = jnp.concatenate(query_parts, 1)
    key_grads = jnp.stack(key_parts, 1)
    value_grads = jnp.stack(value_parts, 1)
    raw_query_grad, raw_key_grad, gain_grad = backward((query_grads, key_grads))
    query_out = raw_query_grad.reshape(tokens, -1).astype(jnp.bfloat16)
    resp_out = jnp.stack(
        [raw_key_grad.reshape(tokens, -1), value_grads.reshape(tokens, -1)], 1
    ).astype(jnp.bfloat16)
    prefix_out = jnp.where(my_index == owner_index, prefix_total, 0.0).astype(jnp.bfloat16)
    gain_total = lax.psum(gain_grad, ("group", "prompts")) / (group_size * lax.axis_size("prompts"))
    return (query_out[None, None], resp_out[None, None], prefix_out[None, None], gain_total)


def solution(mesh):
    return jax.shard_map(
        body,
        mesh=mesh,
        in_specs=(
            P("prompts", "group", None, None),
            P("prompts", "group", None, None, None),
            P("prompts", "group", None, None, None),
            P(),
            P("prompts", "group", None, None),
            P("prompts", "group"),
            P("prompts", "group"),
            P("prompts"),
        ),
        out_specs=(
            P("prompts", "group", None, None),
            P("prompts", "group", None, None, None),
            P("prompts", "group", None, None, None),
            P(),
        ),
        check_vma=False,
    )
```

profile of v0, /device:TPU:1, one launch (start us, length us, event | category | flops | bytes accessed | tf_op | source)
XLA Modules:
  0.0 380.8 jit_solution(1931683212508621535)
XLA Ops:
  7.9 1.9 fusion.42
  13.8 3.3 copy.54
  17.5 3.3 copy.55
  20.9 31.3 %all-reduce.6 = (f32[]{:T(128)}, f32[]{:T(128)}) all-reduce(f32[]{:T(128)} %bitcast.23, f32[]{:T(128)S(6)} %mul.475), channel_id=1, replica_groups=mesh['group'=8,'prompts'=32] {'group'}, use_global_device_ids=true, to_apply=%region_4.5 | all-reduce | flops 2 | bytes 16 | tf_op jit(solution)/shard_map/psum | solution.py:87
  57.8 3.3 copy.57
  61.1 1.7 convert_multiply_fusion
  62.9 4.1 %copy.58 = bf16[256,32,128]{2,0,1:T(8,128)(2,1)} copy(bf16[256,32,128]{0,2,1:T(8,128)(2,1)} %bitcast.251) | data formatting | bytes 4194304 | tf_op jit(solution)/shard_map/mul | solution.py:109
  68.0 4.1 %multiply_multiply_fusion = f32[256,32,128]{2,0,1:T(8,128)S(1)} fusion(f32[256,32,128]{2,0,1:T(8,128)} %copy.55, f32[128]{0:T(128)S(1)} %get-tuple-element.59, f32[256,32]{0,1:T(8,128)S(1)} %fusion.67), kind=kLoop, calls=%fused_computation.29 | loop fusion | flops 2097152 | bytes 8421888 | tf_op jit(solution)/shard_map/jvp()/mul | solution.py:34
  76.1 2.0 select_convert_fusion
  78.0 40.4 %all-reduce.10.cloned.1.call-done = bf16[256,2,512]{2,0,1:T(8,128)(2,1)} async-done(((bf16[256,2,512]{2,0,1:T(8,128)(2,1)}), bf16[256,2,512]{2,0,1:T(8,128)(2,1)}) %all-reduce.10.cloned.1.call-update) | async-done | bytes 524304 | tf_op jit(solution)/shard_map/psum | solution.py:17
  119.5 2.0 fusion.54
  123.3 3.6 fusion.10
  136.9 1.9 fusion.17
  145.6 2.0 fusion.18
  151.3 2.0 fusion.20
  157.5 2.0 fusion.19
  165.0 87.8 %all-reduce.11 = bf16[256,2,512]{2,0,1:T(8,128)(2,1)S(1)} all-reduce(f32[256,2,512]{2,0,1:T(8,128)S(1)} %maximum_maximum_fusion), channel_id=1, replica_groups=mesh['group'=8,'prompts'=32] {'group'}, use_global_device_ids=true, to_apply=%region_11.12 | all-reduce | flops 262144 | bytes 1572864 | tf_op jit(solution)/shard_map/psum | solution.py:135
  259.0 1.9 pad_maximum_fusion
  260.9 1.7 multiply_add_fusion.1
  263.1 3.7 multiply_reduce_fusion
  266.8 92.4 %psum.39 = f32[2,128]{1,0:T(2,128)S(1)} all-reduce(f32[2,128]{1,0:T(2,128)S(1)} %pad_add_fusion.2), channel_id=1, replica_groups=mesh['group'=8,'prompts'=32] {'group','prompts'}, use_global_device_ids=true, to_apply=%region_14.15 | all-reduce | flops 256 | bytes 2048 | tf_op jit(solution)/shard_map/psum | solution.py:145
  359.8 7.8 %fusion = bf16[256,32,128]{2,0,1:T(8,128)(2,1)} fusion(f32[256,32,128]{2,0,1:T(8,128)} %copy.55, f32[256,32]{0,1:T(8,128)S(1)} %multiply_multiply_fusion.2, f32[128]{0:T(128)S(1)} %get-tuple-element.59, f32[256,32]{0,1:T(8,128)S(1)} %copy-done.13, f32[256,32,64]{2,0,1:T(8,128)} %copy-done.4, f32[256,32,64]{2,0,1:T(8,128)} %copy-done.3), kind=kLoop, calls=%fused_computation.1 | loop fusion | flops 7340032 | bytes 10551808 | tf_op jit(solution)/shard_map/convert_element_type | solution.py:140
  367.6 3.3 copy.76
  370.8 2.9 copy.104
  (127 shorter events, 51.1 us)
Async XLA Ops:
  7.2 111.2 %all-reduce.10.cloned.1.call-start = ((), (), s32[]{:S(2)}) async-start(), calls=%async_computation | async-start | bytes 1048576 | tf_op jit(solution)/shard_map/psum | solution.py:17
  17.1 37.7 %copy-start.24 = (f32[2,128]{1,0:T(2,128)S(1)}, f32[2,128]{1,0:T(2,128)}, u32[]{:S(2)}) copy-start(f32[2,128]{1,0:T(2,128)} %param.11) | copy-start | bytes 3076
  17.5 43.5 %copy-start.14 = (f32[256,32]{0,1:T(8,128)}, f32[256,32]{0,1:T(8,128)S(1)}, u32[]{:S(2)}) copy-start(f32[256,32]{0,1:T(8,128)S(1)} %multiply_reduce_fusion.2) | copy-start | bytes 98308
  54.8 12.7 %copy-start.22 = (f32[128]{0:T(128)}, f32[128]{0:T(128)S(1)}, u32[]{:S(2)}) copy-start(f32[128]{0:T(128)S(1)} %get-tuple-element.58) | copy-start | bytes 1540
  57.8 10.2 %copy-start.12 = (f32[256,32]{0,1:T(8,128)}, f32[256,32]{0,1:T(8,128)S(1)}, u32[]{:S(2)}) copy-start(f32[256,32]{0,1:T(8,128)S(1)} %fusion.67) | copy-start | bytes 98308
  73.5 1.4 copy-start
  73.5 1.7 copy-start.25
  73.5 2.5 copy-start.5
  73.5 2.5 copy-start.26
  119.5 2.0 copy-start.1
  123.3 3.6 copy-start.8
  138.8 3.2 copy-start.20
  144.7 2.8 copy-start.19
  150.2 3.0 copy-start.18
  157.5 6.0 %copy-start.10 = (f32[512,128]{1,0:T(8,128)S(1)}, f32[512,128]{1,0:T(8,128)}, u32[]{:S(2)}) copy-start(f32[512,128]{1,0:T(8,128)} %fusion.25) | copy-start | bytes 786436
  157.5 6.7 %copy-start.9 = (f32[512,128]{1,0:T(8,128)S(1)}, f32[512,128]{1,0:T(8,128)}, u32[]{:S(2)}) copy-start(f32[512,128]{1,0:T(8,128)} %fusion.27) | copy-start | bytes 786436
  164.9 90.7 %copy-start.23 = (f32[128]{0:T(128)S(1)}, f32[128]{0:T(128)}, u32[]{:S(2)}) copy-start(f32[128]{0:T(128)} %copy-done.22) | copy-start | bytes 1540
  255.3 3.7 copy-start.6
  255.3 3.7 copy-start.7
  260.9 2.2 copy-start.2
  260.9 2.2 copy-start.13
  262.6 4.2 %copy-start.3 = (f32[256,32,64]{2,0,1:T(8,128)}, f32[256,32,64]{2,0,1:T(8,128)S(1)}, u32[]{:S(2)}) copy-start(f32[256,32,64]{2,0,1:T(8,128)S(1)} %get-tuple-element.22) | copy-start | bytes 6291460
  262.6 4.2 %copy-start.4 = (f32[256,32,64]{2,0,1:T(8,128)}, f32[256,32,64]{2,0,1:T(8,128)S(1)}, u32[]{:S(2)}) copy-start(f32[256,32,64]{2,0,1:T(8,128)S(1)} %get-tuple-element.23) | copy-start | bytes 6291460
  263.1 96.7 %copy-start.15 = (f32[256,32]{0,1:T(8,128)S(1)}, f32[256,32]{0,1:T(8,128)}, u32[]{:S(2)}) copy-start(f32[256,32]{0,1:T(8,128)} %copy-done.14) | copy-start | bytes 98308
  (4 other events, 3.9 us)
Sparse Core Ops, SparseCore 0:
  11.2 107.1 all-reduce.9
where the time goes:
time: 386 us; the launch traced here: 381 us
  blocking collectives  212 us (55%)
  waiting for transfers between devices  40.4 us (10%)
  local copies, waits for them, and re-layouts  38.9 us (10%)
  matrix products  35.6 us (9%)
  other arithmetic  34.9 us (9%)
  between operations  19.5 us (5%)
    psum x1, blocking collectives, body(): lax.psum(gain_grad, ('group', 'prompts'))  92.4 us
    psum x1, blocking collectives, body(): prefix_total = lax.psum(prefix_total, 'group')  87.8 us
    psum x1, waiting for transfers between devices, broadcast(): return lax.psum(block, axis)  40.4 us
    psum x1, blocking collectives, body(): reward_total, square_total = lax.psum((reward, reward * reward), 'group')  31.3 us
    unnamed x68, local copies, waits for them, and re-layouts  21.4 us
    dot_general x4, matrix products, head_grads(): jnp.einsum('gts,sd->tgd', score_grad, head_keys, preferred_element_type=j...  7.86 us
    convert_element_type x1, other arithmetic, body(): query_out = raw_query_grad.reshape(tokens, -1).astype(jnp.bfloat16)  7.77 us
  transfers between devices with their start and end apart: 1, of which 1 were waited for; matrix products, arithmetic and copies ran while one was open for 8% of the time, Pallas kernels for 0%

commit v1 on v0

v1 whole, which is shorter than its diff:
```python
from functools import partial

import jax
import jax.numpy as jnp
import numpy as np
from jax import lax
from jax.experimental import pallas as pl
from jax.experimental.pallas import tpu as pltpu
from jax.sharding import PartitionSpec as P

HD = 128
T = 256
KVH = 4
GW = 8
NX = 4
CH = 64
EPSILON = 1e-06
THETA = 1000000.0
SCALE = HD**-0.5
LOG2E = 1.4426950408889634
LN2 = 0.6931471805599453
SHIFT = 40.0
UNROLL = 4
F32 = jnp.float32
BF = jnp.bfloat16
MESH = pl.DeviceIdType.MESH


def nn(a, b):
    return lax.dot_general(a, b, (((1,), (0,)), ((), ())), preferred_element_type=F32)


def nt(a, b):
    return lax.dot_general(a, b, (((1,), (1,)), ((), ())), preferred_element_type=F32)


def tables():
    positions = T + np.arange(T, dtype=np.float64)
    angles = positions[:, None] * (THETA ** (-2.0 * np.arange(HD // 2) / HD))[None, :]
    c, s = np.cos(angles), np.sin(angles)
    natural = np.stack([np.concatenate([c, c], 1), np.concatenate([-s, s], 1)])
    return natural.astype(np.float32), np.stack([c.T, s.T]).astype(np.float32)


def kernel(
    q_hbm, kv_hbm, px_hbm, gain_ref, do_hbm, len_ref, rew_ref, own_ref, nat_ref, tr_ref,
    dq_hbm, dkv_hbm, dpx_hbm, dg_ref,
    q_vm, do_vm, kv_vm, cot_vm, dq_vm, dkv_vm, dpx_vm,
    qn_s, qc_s, r_s, kall, vall, kt_s, kn_s, rk_s, tabs, amb, dka, dva, gacc, gks,
    e_s, p_s, wb_s, gb_s,
    a_buf, b_buf, c_buf, r_buf, rr_buf, t_buf, tt_buf, tf_buf, ff_buf,
    rw_buf, ga_buf, gb_buf, gc_buf,
    in_sem, out_sem, own_sem,
    p1_s, p1_r, bz_s, bz_r, ag_s, ag_r, rs_s, rs_r, rz_s, rz_r, fg_s, fg_r,
    rw_s, rw_r, ga_s, ga_r, gb2_s, gb2_r, gc_s, gc_r,
):
    me = lax.axis_index("group")
    pr = lax.axis_index("prompts")
    my_x, my_z = lax.rem(me, NX), lax.div(me, NX)
    my_yc, my_zl = lax.rem(pr, 8), lax.div(pr, 8)
    z_peer = {"group": lax.rem(me + NX, 2 * NX)}

    def x_peer(k):
        return {"group": my_z * NX + lax.rem(my_x + k, NX)}

    def g_peer(k):
        return {"group": lax.rem(me + k, 2 * NX)}

    def yc_peer(k):
        return {"prompts": my_zl * 8 + lax.rem(my_yc + k, 8)}

    def zl_peer(k):
        return {"prompts": lax.rem(my_zl + k, 4) * 8 + my_yc}

    def behind(mine, k, n):
        return lax.rem(mine + n - k, n)

    def remote(src, dst, ss, rs, dev):
        return pltpu.make_async_remote_copy(
            src_ref=src, dst_ref=dst, send_sem=ss, recv_sem=rs, device_id=dev, device_id_type=MESH
        )

    barrier = pltpu.get_barrier_semaphore()
    for k in range(1, 8):
        pl.semaphore_signal(barrier, inc=1, device_id=g_peer(k), device_id_type=MESH)
        pl.semaphore_signal(barrier, inc=1, device_id=yc_peer(k), device_id_type=MESH)
    for k in range(1, 4):
        pl.semaphore_signal(barrier, inc=1, device_id=zl_peer(k), device_id_type=MESH)

    def in_copy(kind, g):
        cols = pl.ds(pl.multiple_of(g * (GW * HD), GW * HD), GW * HD)
        src, dst = ((q_hbm, q_vm), (do_hbm, do_vm))[kind]
        return pltpu.make_async_copy(src.at[:, cols], dst.at[:, cols], in_sem.at[kind, g])

    def out_copy(g):
        cols = pl.ds(pl.multiple_of(g * (GW * HD), GW * HD), GW * HD)
        return pltpu.make_async_copy(dq_vm.at[:, cols], dq_hbm.at[:, cols], out_sem.at[g])

    kv_copy = pltpu.make_async_copy(kv_hbm, kv_vm, in_sem.at[2, 0])
    kv_copy.start()
    for g in range(KVH):
        in_copy(0, g).start()
        in_copy(1, g).start()

    rw_buf[me] = jnp.full((8, HD), rew_ref[0, 0].astype(F32), F32)
    gain_t = jnp.broadcast_to(gain_ref[0:1, :], (HD, HD)).T
    gain_t = jnp.concatenate([gain_t, gain_t], 1)
    cos_c, sin_c = tr_ref[0] * (SCALE * LOG2E), tr_ref[1] * (SCALE * LOG2E)
    tabs[0] = gain_t[:64] * cos_c
    tabs[1] = gain_t[64:] * sin_c
    tabs[2] = gain_t[64:] * cos_c
    tabs[3] = gain_t[:64] * sin_c
    gacc[...] = jnp.zeros_like(gacc)
    gks[...] = jnp.zeros_like(gks)
    gk = gain_ref[1:2, :]
    tri = lax.broadcasted_iota(jnp.int32, (HD, HD), 0) <= lax.broadcasted_iota(jnp.int32, (HD, HD), 1)
    owner = own_ref[0]
    owner_x, owner_z = lax.rem(owner, NX), lax.div(owner, NX)

    pl.semaphore_wait(barrier, 17)

    def head_cols(g):
        return pl.ds(pl.multiple_of(g * HD, HD), HD)

    def rows(x):
        return pl.ds(pl.multiple_of(x * CH, CH), CH)

    def rw_copy(k, slot):
        return remote(rw_buf.at[me], rw_buf.at[slot], rw_s.at[k], rw_r.at[k], g_peer(k))

    for k in range(1, 8):
        rw_copy(k, me).start()

    def p1_copy(g, k, slot):
        src = px_hbm.at[rows(lax.rem(my_x + k, NX)), :, head_cols(g)]
        return remote(src, a_buf[g].at[slot], p1_s.at[g, k], p1_r.at[g, k], x_peer(k))

    def own_copy(g):
        return pltpu.make_async_copy(px_hbm.at[rows(my_x), :, head_cols(g)], a_buf[g].at[my_x], own_sem.at[g])

    def bz_copy(g, slot):
        return remote(b_buf[g].at[my_z], b_buf[g].at[slot], bz_s.at[g], bz_r.at[g], z_peer)

    def ag_copy(g, k, x):
        return remote(c_buf.at[g, rows(my_x)], c_buf.at[g, rows(x)], ag_s.at[g, k], ag_r.at[g, k], x_peer(k))

    for g in range(KVH):
        for k in range(1, NX):
            p1_copy(g, k, my_x).start()
        own_copy(g).start()

    def bc1(g):
        own_copy(g).wait()
        for k in range(1, NX):
            p1_copy(g, k, behind(my_x, k, NX)).wait_recv()
        b_buf[g][my_z] = a_buf[g][owner_x]
        bz_copy(g, my_z).start()

    def bc2(g):
        bz_copy(g, 1 - my_z).wait_recv()
        c_buf[g, rows(my_x)] = b_buf[g][owner_z]
        for k in range(1, NX):
            ag_copy(g, k, my_x).start()

    def bc3(g):
        for k in range(1, NX):
            ag_copy(g, k, behind(my_x, k, NX)).wait_recv()
        kall[g, 0:T] = c_buf[g, :, 0, :]
        vall[g, 0:T] = c_buf[g, :, 1, :]
        kt_s[g] = kall[g].T

    def rs_copy(g, k, slot):
        src = r_buf.at[g, rows(lax.rem(my_x + k, NX))]
        return remote(src, rr_buf.at[g, slot], rs_s.at[g, k], rs_r.at[g, k], x_peer(k))

    def rz_copy(g):
        return remote(t_buf.at[g], tt_buf.at[g], rz_s.at[g], rz_r.at[g], z_peer)

    def fg_copy(g, k, x):
        return remote(ff_buf.at[g, rows(my_x)], ff_buf.at[g, rows(x)], fg_s.at[g, k], fg_r.at[g, k], x_peer(k))

    def rd1(g):
        r_buf[g, :, 0:HD] = (dka[0:T] * LN2).astype(BF)
        r_buf[g, :, HD:] = dva[0:T].astype(BF)
        tf_buf[g, :, 0:HD] = dka[rows(my_x)] * LN2
        tf_buf[g, :, HD:] = dva[rows(my_x)]
        for k in range(1, NX):
            rs_copy(g, k, my_x).start()

    def rd2(g):
        total = tf_buf[g]
        for k in range(1, NX):
            rs_copy(g, k, behind(my_x, k, NX)).wait_recv()
            total = total + rr_buf[g, behind(my_x, k, NX)].astype(F32)
        tf_buf[g] = total
        t_buf[g] = total.astype(BF)
        rz_copy(g).start()

    def rd3(g):
        rz_copy(g).wait_recv()
        ff_buf[g, rows(my_x)] = (tf_buf[g] + tt_buf[g].astype(F32)).astype(BF)
        for k in range(1, NX):
            fg_copy(g, k, my_x).start()

    def rd4(g):
        for k in range(1, NX):
            fg_copy(g, k, behind(my_x, k, NX)).wait_recv()
        mine = owner == me
        cols = head_cols(g)
        dpx_vm[:, 0, cols] = jnp.where(mine, ff_buf[g, :, 0:HD], jnp.zeros((T, HD), BF))
        dpx_vm[:, 1, cols] = jnp.where(mine, ff_buf[g, :, HD:], jnp.zeros((T, HD), BF))

    kv_copy.wait()

    def key_prep(g, _):
        cols = head_cols(g)
        raw = kv_vm[:, 0, cols].astype(F32)
        rk = lax.rsqrt(jnp.mean(raw * raw, -1, keepdims=True) + EPSILON)
        kn = raw * rk
        kn_s[g] = kn
        rk_s[g] = jnp.broadcast_to(rk, (T, HD))
        kg = kn * gk
        kall[g, T : 2 * T] = (kg * nat_ref[0] + pltpu.roll(kg, HD // 2, 1) * nat_ref[1]).astype(BF)
        vall[g, T : 2 * T] = kv_vm[:, 1, cols]
        return 0

    lax.fori_loop(0, KVH, key_prep, 0)

    for k in range(1, 8):
        rw_copy(k, behind(me, k, 8)).wait_recv()
    total = rw_buf[0]
    square = rw_buf[0] * rw_buf[0]
    for k in range(1, 8):
        total = total + rw_buf[k]
        square = square + rw_buf[k] * rw_buf[k]
    mean = total / 8
    spread = jnp.sqrt(jnp.maximum(square / 8 - mean * mean, 0.0))
    advantage = (rw_buf[me] - mean) / jnp.maximum(spread, 1.0)
    live = lax.broadcasted_iota(jnp.int32, (T, HD), 0) < len_ref[0, 0]
    amb[...] = jnp.where(live, jnp.broadcast_to(advantage[0:1, :], (T, HD)), 0.0)

    def query_prep(g):
        in_copy(0, g).wait()
        in_copy(1, g).wait()

        def one(h):
            cols = head_cols(h)
            cot_vm[:, cols] = (do_vm[:, cols].astype(F32) * amb[...]).astype(BF)
            x = q_vm[:, cols].T.astype(F32)
            r = lax.rsqrt(jnp.sum(x * x, 0, keepdims=True) * (1.0 / HD) + EPSILON)
            qn = x * r
            qa, qb = qn[:64], qn[64:]
            r_s[h] = jnp.broadcast_to(r, (8, T))
            qn_s[h] = qn
            qc_s[h, 0:64] = (qa * tabs[0] - qb * tabs[1]).astype(BF)
            qc_s[h, 64:HD] = (qb * tabs[2] + qa * tabs[3]).astype(BF)

        def some(i, _):
            for j in range(UNROLL):
                one(g * GW + i * UNROLL + j)
            return 0

        lax.fori_loop(0, GW // UNROLL, some, 0)

    query_prep(0)
    bc1(0)
    query_prep(1)
    bc1(1)
    bc2(0)
    query_prep(2)
    bc1(2)
    bc2(1)
    query_prep(3)
    bc1(3)
    bc2(2)
    bc2(3)

    def head(g, h, slot):
        cols = head_cols(h)
        cot = cot_vm[:, cols]
        qc = qc_s[h]
        e_r, p_r, wb_r, gb_r = e_s.at[slot], p_s.at[slot], wb_s.at[slot], gb_s.at[slot]
        sum_e = jnp.zeros((8, T), F32)
        sum_ep = jnp.zeros((8, T), F32)
        for s0 in range(0, 2 * T, HD):
            block = slice(s0, s0 + HD)
            scores = nn(kall[g, block], qc)
            prob = nt(vall[g, block], cot)
            e = jnp.exp2(scores - SHIFT)
            if s0 == T:
                e = jnp.concatenate([jnp.where(tri, e[:, :HD], 0.0), e[:, HD:]], 1)
            elif s0 == T + HD:
                e = jnp.concatenate([jnp.zeros((HD, HD), F32), jnp.where(tri, e[:, HD:], 0.0)], 1)
            e_r[block] = e
            p_r[block] = prob
            sum_e = sum_e + jnp.sum(e.reshape(HD // 8, 8, T), 0)
            sum_ep = sum_ep + jnp.sum((e * prob).reshape(HD // 8, 8, T), 0)
        inv = 1.0 / jnp.sum(sum_e, 0, keepdims=True)
        dots = jnp.sum(sum_ep, 0, keepdims=True) * inv
        for s0 in range(0, 2 * T, HD):
            block = slice(s0, s0 + HD)
            w = e_r[block] * inv
            wb_r[block] = w.astype(BF)
            gb_r[block] = (w * (p_r[block] - dots)).astype(BF)
        dva[...] += nn(wb_r[...], cot)
        dka[...] += nt(gb_r[...], qc)
        dt = nn(kt_s[g], gb_r[...])
        da, db = dt[:64], dt[64:]
        va = da * tabs[0] + db * tabs[3]
        vb = db * tabs[2] - da * tabs[1]
        qa, qb = qn_s[h, 0:64], qn_s[h, 64:HD]
        pa, pb = va * qa, vb * qb
        gacc[0:64] += pa
        gacc[64:HD] += pb
        m = (jnp.sum(pa, 0, keepdims=True) + jnp.sum(pb, 0, keepdims=True)) * (1.0 / HD)
        r = r_s[h, 0:1] * LN2
        dx = jnp.concatenate([(va - qa * m) * r, (vb - qb * m) * r], 0).astype(BF)
        dq_vm[:, cols] = dx.T

    def key_head(g, _):
        bc3(g)
        dka[...] = jnp.zeros_like(dka)
        dva[...] = jnp.zeros_like(dva)

        def some(i, _):
            for j in range(UNROLL):
                head(g, g * GW + i * UNROLL + j, j)

            @pl.when((g > 0) & (i == 0))
            def _():
                rd2(g - 1)

            @pl.when((g > 0) & (i == 1))
            def _():
                rd3(g - 1)

            return 0

        lax.fori_loop(0, GW // UNROLL, some, 0)
        rd1(g)
        out_copy(g).start()
        cols = head_cols(g)
        dk = dka[T : 2 * T] * LN2
        u = dk * nat_ref[0] - pltpu.roll(dk, HD // 2, 1) * nat_ref[1]
        kn = kn_s[g]
        gks[0:1] += jnp.sum(u * kn, 0, keepdims=True)
        v = u * gk
        m = jnp.mean(v * kn, -1, keepdims=True)
        dkv_vm[:, 0, cols] = (rk_s[g] * (v - kn * m)).astype(BF)
        dkv_vm[:, 1, cols] = dva[T : 2 * T].astype(BF)
        return 0

    lax.fori_loop(0, KVH, key_head, 0)

    def stage(buf, mine, n, peer, ss, rs):
        def copy(k, slot):
            return remote(buf.at[mine], buf.at[slot], ss.at[k], rs.at[k], peer(k))

        def start():
            for k in range(1, n):
                copy(k, mine).start()

        def finish():
            for k in range(1, n):
                copy(k, behind(mine, k, n)).wait_recv()
            out = buf[0]
            for k in range(1, n):
                out = out + buf[k]
            return out

        def drain():
            for k in range(1, n):
                copy(k, mine).wait_send()

        return start, finish, drain

    ga_start, ga_finish, ga_drain = stage(ga_buf, me, 8, g_peer, ga_s, ga_r)
    gb_start, gb_finish, gb_drain = stage(gb_buf, my_yc, 8, yc_peer, gb2_s, gb2_r)
    gc_start, gc_finish, gc_drain = stage(gc_buf, my_zl, 4, zl_peer, gc_s, gc_r)

    dkv_copy = pltpu.make_async_copy(dkv_vm, dkv_hbm, out_sem.at[4])
    dkv_copy.start()
    gq = jnp.broadcast_to(jnp.sum(gacc[...], 1, keepdims=True), (HD, HD)).T * LN2 / gain_ref[0:1, :]
    ga_buf[me] = jnp.concatenate([gq[0:1], gks[0:1], jnp.zeros((6, HD), F32)], 0)
    ga_start()
    rd2(KVH - 1)
    gb_buf[my_yc] = ga_finish()
    gb_start()
    rd3(KVH - 1)
    gc_buf[my_zl] = gb_finish()
    gc_start()
    for g in range(KVH):
        rd4(g)
    dpx_copy = pltpu.make_async_copy(dpx_vm, dpx_hbm, out_sem.at[5])
    dpx_copy.start()
    dg_ref[...] = gc_finish()[0:2] * (1.0 / 256)

    for k in range(1, 8):
        rw_copy(k, me).wait_send()
    ga_drain()
    gb_drain()
    gc_drain()
    for g in range(KVH):
        bz_copy(g, my_z).wait_send()
        rz_copy(g).wait_send()
        for k in range(1, NX):
            p1_copy(g, k, my_x).wait_send()
            ag_copy(g, k, my_x).wait_send()
            rs_copy(g, k, my_x).wait_send()
            fg_copy(g, k, my_x).wait_send()
        out_copy(g).wait()
    dkv_copy.wait()
    dpx_copy.wait()


def body(queries, resp_kv, prefix_kv, norm_gains, dout, lengths, rewards, owner):
    natural, transposed = tables()
    anywhere = pl.BlockSpec(memory_space=pl.ANY)
    vmem = pl.BlockSpec(memory_space=pltpu.VMEM)
    smem = pl.BlockSpec(memory_space=pltpu.SMEM)
    dma = pltpu.SemaphoreType.DMA
    out = pl.pallas_call(
        kernel,
        out_shape=[
            jax.ShapeDtypeStruct((T, 4096), BF),
            jax.ShapeDtypeStruct((T, 2, 512), BF),
            jax.ShapeDtypeStruct((T, 2, 512), BF),
            jax.ShapeDtypeStruct((2, HD), F32),
        ],
        in_specs=[anywhere, anywhere, anywhere, vmem, anywhere, smem, smem, smem, vmem, vmem],
        out_specs=[anywhere, anywhere, anywhere, vmem],
        scratch_shapes=[
            pltpu.VMEM((T, 4096), BF),
            pltpu.VMEM((T, 4096), BF),
            pltpu.VMEM((T, 2, 512), BF),
            pltpu.VMEM((T, 4096), BF),
            pltpu.VMEM((T, 4096), BF),
            pltpu.VMEM((T, 2, 512), BF),
            pltpu.VMEM((T, 2, 512), BF),
            pltpu.VMEM((32, HD, T), F32),
            pltpu.VMEM((32, HD, T), BF),
            pltpu.VMEM((32, 8, T), F32),
            pltpu.VMEM((KVH, 2 * T, HD), BF),
            pltpu.VMEM((KVH, 2 * T, HD), BF),
            pltpu.VMEM((KVH, HD, 2 * T), BF),
            pltpu.VMEM((KVH, T, HD), F32),
            pltpu.VMEM((KVH, T, HD), F32),
            pltpu.VMEM((4, HD // 2, T), F32),
            pltpu.VMEM((T, HD), F32),
            pltpu.VMEM((2 * T, HD), F32),
            pltpu.VMEM((2 * T, HD), F32),
            pltpu.VMEM((HD, T), F32),
            pltpu.VMEM((8, HD), F32),
            pltpu.VMEM((UNROLL, 2 * T, T), F32),
            pltpu.VMEM((UNROLL, 2 * T, T), F32),
            pltpu.VMEM((UNROLL, 2 * T, T), BF),
            pltpu.VMEM((UNROLL, 2 * T, T), BF),
            [pltpu.VMEM((NX, CH, 2, HD), BF)] * KVH,
            [pltpu.VMEM((2, CH, 2, HD), BF)] * KVH,
            pltpu.VMEM((KVH, T, 2, HD), BF),
            pltpu.VMEM((KVH, T, 2 * HD), BF),
            pltpu.VMEM((KVH, NX, CH, 2 * HD), BF),
            pltpu.VMEM((KVH, CH, 2 * HD), BF),
            pltpu.VMEM((KVH, CH, 2 * HD), BF),
            pltpu.VMEM((KVH, CH, 2 * HD), F32),
            pltpu.VMEM((KVH, T, 2 * HD), BF),
            pltpu.VMEM((8, 8, HD), F32),
            pltpu.VMEM((8, 8, HD), F32),
            pltpu.VMEM((8, 8, HD), F32),
            pltpu.VMEM((4, 8, HD), F32),
            dma((3, KVH)),
            dma((6,)),
            dma((KVH,)),
            dma((KVH, NX)),
            dma((KVH, NX)),
            dma((KVH,)),
            dma((KVH,)),
            dma((KVH, NX)),
            dma((KVH, NX)),
            dma((KVH, NX)),
            dma((KVH, NX)),
            dma((KVH,)),
            dma((KVH,)),
            dma((KVH, NX)),
            dma((KVH, NX)),
            dma((8,)),
            dma((8,)),
            dma((8,)),
            dma((8,)),
            dma((8,)),
            dma((8,)),
            dma((4,)),
            dma((4,)),
        ],
        compiler_params=pltpu.CompilerParams(
            collective_id=0, has_side_effects=True, vmem_limit_bytes=48 << 20
        ),
    )(
        queries[0, 0], resp_kv[0, 0], prefix_kv[0, 0], norm_gains, dout[0, 0],
        lengths, rewards, owner, natural, transposed,
    )
    return (out[0][None, None], out[1][None, None], out[2][None, None], out[3])


def solution(mesh):
    return jax.shard_map(
        body,
        mesh=mesh,
        in_specs=(
            P("prompts", "group", None, None),
            P("prompts", "group", None, None, None),
            P("prompts", "group", None, None, None),
            P(),
            P("prompts", "group", None, None),
            P("prompts", "group"),
            P("prompts", "group"),
            P("prompts"),
        ),
        out_specs=(
            P("prompts", "group", None, None),
            P("prompts", "group", None, None, None),
            P("prompts", "group", None, None, None),
            P(),
        ),
        check_vma=False,
    )
```

time: 386 us -> 90.2 us (0.23); the launches traced: 381 us -> 89.9 us
  blocking collectives: 212 us -> 0 us
  Pallas kernels: 0 us -> 79.3 us
  waiting for transfers between devices: 40.4 us -> 0 us
  matrix products: 35.6 us -> 0 us
  other arithmetic: 34.9 us -> 0 us
  local copies, waits for them, and re-layouts: 38.9 us -> 8.08 us
  between operations: 19.5 us -> 2.59 us
    psum x3 -> x0, blocking collectives: 212 us -> none  [the longest x1 92.4 us: body(): lax.psum(gain_grad, ('group', 'prompts'))]
    pallas_call x0 -> x1, Pallas kernels: none -> 79.3 us  [body(): pl.pallas_call(kernel, out_shape=[jax.ShapeDtypeStruct((T, 4096), BF), ja...]
    psum x1 -> x0, waiting for transfers between devices: 40.4 us -> none  [broadcast(): return lax.psum(block, axis)]
    dot_general x24 -> x0, matrix products: 35.6 us -> none  [the longest x4 7.86 us: head_grads(): jnp.einsum('gts,sd->tgd', score_grad, head_keys, preferred_element_type=j...]
    unnamed x68 -> x14, local copies, waits for them, and re-layouts: 21.4 us -> 8.08 us
    convert_element_type x2 -> x0, other arithmetic: 9.73 us -> none  [the longest x1 7.77 us: body(): query_out = raw_query_grad.reshape(tokens, -1).astype(jnp.bfloat16)]
    convert_element_type x3 -> x0, local copies, waits for them, and re-layouts: 6.74 us -> none  [the longest x1 3.34 us: body(): local_queries.astype(jnp.float32).reshape(tokens, query_heads, HD)]
    mul x3 -> x0, other arithmetic: 6.02 us -> none  [the longest x2 4.29 us: normalize(): values * lax.rsqrt(jnp.mean(values * values, -1, keepdims=True) + EPSILON)]
  transfers between devices with their start and end apart: 1 -> 0, of which waited for: 1 -> 0; matrix products, arithmetic and copies ran while one was open for 8% -> 0% of each run, Pallas kernels for 0% -> 0%
where the time goes in v1:
time: 90.2 us; the launch traced here: 89.9 us
  Pallas kernels  79.3 us (88%)
  local copies, waits for them, and re-layouts  8.08 us (9%)
  between operations  2.59 us (3%)
    pallas_call x1, Pallas kernels, body(): pl.pallas_call(kernel, out_shape=[jax.ShapeDtypeStruct((T, 4096), BF), ja...  79.3 us
    unnamed x14, local copies, waits for them, and re-layouts  8.08 us

profile of v1, /device:TPU:1, one launch (start us, length us, event | category | flops | bytes accessed | tf_op | source)
XLA Modules:
  0.0 89.9 jit_solution(12224031751071028014)
XLA Ops:
  2.6 0.0 copy-start
  2.6 1.0 %copy-done = bf16[1,1,256,2,512]{4,3,2,1,0:T(2,128)(2,1)S(1)} copy-done((bf16[1,1,256,2,512]{4,3,2,1,0:T(2,128)(2,1)S(1)}, bf16[1,1,256,2,512]{4,3,2,1,0:T(2,128)(2,1)}, u32[]{:S(2)}) %copy-start) | copy-done | bytes 524312
  3.6 0.0 copy-start.1
  3.6 1.0 %copy-done.1 = bf16[1,1,256,2,512]{4,3,2,1,0:T(2,128)(2,1)S(1)} copy-done((bf16[1,1,256,2,512]{4,3,2,1,0:T(2,128)(2,1)S(1)}, bf16[1,1,256,2,512]{4,3,2,1,0:T(2,128)(2,1)}, u32[]{:S(2)}) %copy-start.1) | copy-done | bytes 524312
  4.7 0.0 copy-start.2
  4.7 0.9 %copy-done.2 = f32[2,256,128]{2,1,0:T(8,128)S(1)} copy-done((f32[2,256,128]{2,1,0:T(8,128)S(1)}, f32[2,256,128]{2,1,0:T(8,128)}, u32[]{:S(2)}) %copy-start.2) | copy-done | bytes 262168
  5.6 0.0 copy-start.3
  5.6 0.9 %copy-done.3 = f32[2,64,256]{2,1,0:T(8,128)S(1)} copy-done((f32[2,64,256]{2,1,0:T(8,128)S(1)}, f32[2,64,256]{2,1,0:T(8,128)}, u32[]{:S(2)}) %copy-start.3) | copy-done | bytes 131096
  6.5 0.0 copy-start.4
  6.5 0.7 copy-done.4
  7.2 79.3 %shard_map.129 = (bf16[256,4096]{1,0:T(8,128)(2,1)S(1)}, bf16[256,2,512]{2,1,0:T(2,128)(2,1)S(1)}, bf16[256,2,512]{2,1,0:T(2,128)(2,1)S(1)}, f32[2,128]{1,0:T(2,128)S(1)}) custom-call(bf16[256,4096]{1,0:T(8,128)(2,1)} %bitcast.12, bf16[256,2,512]{2,1,0:T(2,128)(2,1)S(1)} %bitcast.10, bf16[256,2,512]{2,1,0:T(2,128)(2,1)S(1)} %bitcast.11, ...), custom_call_target="tpu_custom_call" | custom-call | tf_op jit(solution)/shard_map/pallas_call | solution.py:422
  86.5 1.3 %copy.21 = bf16[1,1,256,4096]{3,2,1,0:T(8,128)(2,1)} copy(bf16[1,1,256,4096]{3,2,1,0:T(8,128)(2,1)S(1)} %bitcast.7) | data formatting | bytes 4194304
  87.8 0.8 copy.22
  88.6 0.8 copy.23
  89.4 0.6 copy.24
Async XLA Ops:
  2.6 1.0 %copy-start = (bf16[1,1,256,2,512]{4,3,2,1,0:T(2,128)(2,1)S(1)}, bf16[1,1,256,2,512]{4,3,2,1,0:T(2,128)(2,1)}, u32[]{:S(2)}) copy-start(bf16[1,1,256,2,512]{4,3,2,1,0:T(2,128)(2,1)} %param.11) | copy-start | bytes 1572868
  3.6 1.0 %copy-start.1 = (bf16[1,1,256,2,512]{4,3,2,1,0:T(2,128)(2,1)S(1)}, bf16[1,1,256,2,512]{4,3,2,1,0:T(2,128)(2,1)}, u32[]{:S(2)}) copy-start(bf16[1,1,256,2,512]{4,3,2,1,0:T(2,128)(2,1)} %param.12) | copy-start | bytes 1572868
  4.7 0.9 %copy-start.2 = (f32[2,256,128]{2,1,0:T(8,128)S(1)}, f32[2,256,128]{2,1,0:T(8,128)}, u32[]{:S(2)}) copy-start(f32[2,256,128]{2,1,0:T(8,128)} %constant.4.clone.nat_ref) | copy-start | bytes 786436
  5.6 0.9 %copy-start.3 = (f32[2,64,256]{2,1,0:T(8,128)S(1)}, f32[2,64,256]{2,1,0:T(8,128)}, u32[]{:S(2)}) copy-start(f32[2,64,256]{2,1,0:T(8,128)} %constant.5.clone.tr_ref) | copy-start | bytes 393220
  6.5 0.7 copy-start.4

commit v2 on v1

v2 whole, which is shorter than its diff:
```python
from functools import partial

import jax
import jax.numpy as jnp
import numpy as np
from jax import lax
from jax.experimental import pallas as pl
from jax.experimental.pallas import tpu as pltpu
from jax.sharding import PartitionSpec as P

HD = 128
T = 256
KVH = 4
GW = 8
NX = 4
CH = 64
EPSILON = 1e-06
THETA = 1000000.0
SCALE = HD**-0.5
LOG2E = 1.4426950408889634
LN2 = 0.6931471805599453
SHIFT = 40.0
UNROLL = 4
F32 = jnp.float32
BF = jnp.bfloat16
MESH = pl.DeviceIdType.MESH


def nn(a, b):
    return lax.dot_general(a, b, (((1,), (0,)), ((), ())), preferred_element_type=F32)


def nt(a, b):
    return lax.dot_general(a, b, (((1,), (1,)), ((), ())), preferred_element_type=F32)


def tables():
    positions = T + np.arange(T, dtype=np.float64)
    angles = positions[:, None] * (THETA ** (-2.0 * np.arange(HD // 2) / HD))[None, :]
    c, s = np.cos(angles), np.sin(angles)
    natural = np.stack([np.concatenate([c, c], 1), np.concatenate([-s, s], 1)])
    return natural.astype(np.float32), np.stack([c.T, s.T]).astype(np.float32)


def kernel(
    q_hbm, kv_hbm, px_hbm, gain_hbm, do_hbm, len_hbm, rew_hbm, own_hbm, nat_hbm, tr_hbm,
    dq_hbm, dkv_hbm, dpx_hbm, dg_ref,
    gain_ref, nat_ref, tr_ref, len_ref, rew_ref, own_ref,
    q_vm, do_vm, kv_vm, dkv_vm, dpx_vm,
    qn_s, qc_s, r_s, er_s, pr_s, se_s, sp_s, wr_s, kall, vall, kt_s, kn_s, rk_s, tabs, mask_s, adv_s,
    dkp, dkr, dva, gacc, gks,
    e_s, p_s, wb_s, gb_s,
    a_buf, b_buf, c_buf, r_buf, rr_buf, t_buf, tt_buf, tf_buf, ff_buf,
    rw_buf, ga_buf, gb_buf,
    in_sem, small_sem, out_sem, own_sem,
    p1_s, p1_r, bz_s, bz_r, ag_s, ag_r, rs_s, rs_r, rz_s, rz_r, fg_s, fg_r,
    rw_s, rw_r, ga_s, ga_r, gb2_s, gb2_r,
):
    me = lax.axis_index("group")
    pr = lax.axis_index("prompts")
    my_x, my_z = lax.rem(me, NX), lax.div(me, NX)
    my_core, my_y, my_zl = lax.rem(pr, 2), lax.rem(lax.div(pr, 2), 4), lax.div(pr, 8)
    my_a = my_x * 4 + my_y
    my_b = (my_z * 4 + my_zl) * 2 + my_core
    z_peer = {"group": lax.rem(me + NX, 2 * NX), "prompts": pr}

    def x_peer(k):
        return {"group": my_z * NX + lax.rem(my_x + k, NX), "prompts": pr}

    def g_peer(k):
        return {"group": lax.rem(me + k, 2 * NX), "prompts": pr}

    def a_peer(k):
        a = lax.rem(my_a + k, 16)
        return {"group": my_z * 4 + lax.div(a, 4), "prompts": (my_zl * 4 + lax.rem(a, 4)) * 2 + my_core}

    def b_peer(k):
        b = lax.rem(my_b + k, 16)
        z = lax.div(b, 2)
        return {"group": lax.div(z, 4) * 4 + my_x, "prompts": (lax.rem(z, 4) * 4 + my_y) * 2 + lax.rem(b, 2)}

    def behind(mine, k, n):
        return lax.rem(mine + n - k, n)

    def remote(src, dst, ss, rs, dev):
        return pltpu.make_async_remote_copy(
            src_ref=src, dst_ref=dst, send_sem=ss, recv_sem=rs, device_id=dev, device_id_type=MESH
        )

    def greet(dev):
        pl.semaphore_signal(barrier, inc=1, device_id=dev, device_id_type=MESH)

    barrier = pltpu.get_barrier_semaphore()
    for k in range(1, 16):
        greet(b_peer(k))
        greet(a_peer(k))
    for k in range(1, NX):
        greet({"group": (1 - my_z) * NX + lax.rem(my_x + k, NX), "prompts": pr})

    small = (
        (kv_hbm, kv_vm), (nat_hbm, nat_ref), (tr_hbm, tr_ref), (gain_hbm, gain_ref),
        (len_hbm, len_ref), (rew_hbm, rew_ref), (own_hbm, own_ref),
    )
    small_copies = [pltpu.make_async_copy(a, b, small_sem.at[i]) for i, (a, b) in enumerate(small)]

    def wide(g):
        return pl.ds(pl.multiple_of(g * (GW * HD), GW * HD), GW * HD)

    def in_copy(kind, g):
        src, dst = ((q_hbm, q_vm), (do_hbm, do_vm))[kind]
        return pltpu.make_async_copy(src.at[:, wide(g)], dst.at[:, wide(g)], in_sem.at[kind, g])

    def out_copy(g):
        return pltpu.make_async_copy(q_vm.at[:, wide(g)], dq_hbm.at[:, wide(g)], out_sem.at[g])

    for copy in small_copies:
        copy.start()
    for g in range(KVH):
        in_copy(0, g).start()
        in_copy(1, g).start()
    for copy in small_copies:
        copy.wait()

    rw_buf[me] = jnp.full((8, HD), rew_ref[0, 0].astype(F32), F32)
    gain_t = jnp.broadcast_to(gain_ref[0:1, :], (HD, HD)).T
    gain_t = jnp.concatenate([gain_t, gain_t], 1)
    cos_c, sin_c = tr_ref[0] * (SCALE * LOG2E), tr_ref[1] * (SCALE * LOG2E)
    tabs[0] = gain_t[:64] * cos_c
    tabs[1] = gain_t[64:] * sin_c
    tabs[2] = gain_t[64:] * cos_c
    tabs[3] = gain_t[:64] * sin_c
    gacc[...] = jnp.zeros_like(gacc)
    gks[...] = jnp.zeros_like(gks)
    gk = gain_ref[1:2, :]
    mask_s[...] = jnp.where(lax.broadcasted_iota(jnp.int32, (8, T), 1) < len_ref[0, 0], 1.0, 0.0)
    tri = lax.broadcasted_iota(jnp.int32, (HD, HD), 0) <= lax.broadcasted_iota(jnp.int32, (HD, HD), 1)
    owner = own_ref[0]
    owner_x, owner_z = lax.rem(owner, NX), lax.div(owner, NX)

    def head_cols(g):
        return pl.ds(pl.multiple_of(g * HD, HD), HD)

    def rows(x):
        return pl.ds(pl.multiple_of(x * CH, CH), CH)

    def rw_copy(k, slot):
        return remote(rw_buf.at[me], rw_buf.at[slot], rw_s.at[k], rw_r.at[k], g_peer(k))

    def p1_copy(g, k, slot):
        src = px_hbm.at[rows(lax.rem(my_x + k, NX)), :, head_cols(g)]
        return remote(src, a_buf[g].at[slot], p1_s.at[g, k], p1_r.at[g, k], x_peer(k))

    def own_copy(g):
        return pltpu.make_async_copy(px_hbm.at[rows(my_x), :, head_cols(g)], a_buf[g].at[my_x], own_sem.at[g])

    def bz_copy(g, slot):
        return remote(b_buf[g].at[my_z], b_buf[g].at[slot], bz_s.at[g], bz_r.at[g], z_peer)

    def ag_copy(g, k, x):
        return remote(c_buf.at[g, rows(my_x)], c_buf.at[g, rows(x)], ag_s.at[g, k], ag_r.at[g, k], x_peer(k))

    def bc1(g):
        own_copy(g).wait()
        for k in range(1, NX):
            p1_copy(g, k, behind(my_x, k, NX)).wait_recv()
        b_buf[g][my_z] = a_buf[g][owner_x]
        bz_copy(g, my_z).start()

    def bc2(g):
        bz_copy(g, 1 - my_z).wait_recv()
        c_buf[g, rows(my_x)] = b_buf[g][owner_z]
        for k in range(1, NX):
            ag_copy(g, k, my_x).start()

    def bc3(g):
        for k in range(1, NX):
            ag_copy(g, k, behind(my_x, k, NX)).wait_recv()
        kall[g, 0:T] = c_buf[g, :, 0, :]
        vall[g, 0:T] = c_buf[g, :, 1, :]
        kt_s[g] = kall[g].T

    def rs_copy(g, k, slot):
        src = r_buf.at[g, rows(lax.rem(my_x + k, NX))]
        return remote(src, rr_buf.at[g, slot], rs_s.at[g, k], rs_r.at[g, k], x_peer(k))

    def rz_copy(g):
        return remote(t_buf.at[g], tt_buf.at[g], rz_s.at[g], rz_r.at[g], z_peer)

    def fg_copy(g, k, x):
        return remote(ff_buf.at[g, rows(my_x)], ff_buf.at[g, rows(x)], fg_s.at[g, k], fg_r.at[g, k], x_peer(k))

    def rd1(g):
        adv = adv_s[0:1, 0:HD]
        r_buf[g, :, 0:HD] = (dkp[...] * (adv * LN2)).astype(BF)
        r_buf[g, :, HD:] = (dva[...] * adv).astype(BF)
        for k in range(1, NX):
            rs_copy(g, k, my_x).start()
        tf_buf[g, :, 0:HD] = dkp[rows(my_x)] * (adv * LN2)
        tf_buf[g, :, HD:] = dva[rows(my_x)] * adv

    def rd2(g):
        total = tf_buf[g]
        for k in range(1, NX):
            rs_copy(g, k, behind(my_x, k, NX)).wait_recv()
            total = total + rr_buf[g, behind(my_x, k, NX)].astype(F32)
        tf_buf[g] = total
        t_buf[g] = total.astype(BF)
        rz_copy(g).start()

    def rd3(g):
        rz_copy(g).wait_recv()
        ff_buf[g, rows(my_x)] = (tf_buf[g] + tt_buf[g].astype(F32)).astype(BF)
        for k in range(1, NX):
            fg_copy(g, k, my_x).start()

    def rd4(g):
        for k in range(1, NX):
            fg_copy(g, k, behind(my_x, k, NX)).wait_recv()
        mine = owner == me
        cols = head_cols(g)
        dpx_vm[:, 0, cols] = jnp.where(mine, ff_buf[g, :, 0:HD], jnp.zeros((T, HD), BF))
        dpx_vm[:, 1, cols] = jnp.where(mine, ff_buf[g, :, HD:], jnp.zeros((T, HD), BF))

    def key_prep(g, _):
        cols = head_cols(g)
        raw = kv_vm[:, 0, cols].astype(F32)
        rk = lax.rsqrt(jnp.mean(raw * raw, -1, keepdims=True) + EPSILON)
        kn = raw * rk
        kn_s[g] = kn
        rk_s[g] = jnp.broadcast_to(rk, (T, HD))
        kg = kn * gk
        kall[g, T : 2 * T] = (kg * nat_ref[0] + pltpu.roll(kg, HD // 2, 1) * nat_ref[1]).astype(BF)
        vall[g, T : 2 * T] = kv_vm[:, 1, cols]
        return 0

    lax.fori_loop(0, KVH, key_prep, 0)

    def first_part(g, h):
        cols = head_cols(h)
        cot = do_vm[:, cols]
        x = q_vm[:, cols].T.astype(F32)
        r = lax.rsqrt(jnp.sum(x * x, 0, keepdims=True) * (1.0 / HD) + EPSILON)
        qn = x * r
        qa, qb = qn[:64], qn[64:]
        r_s[h] = jnp.broadcast_to(r, (8, T))
        qn_s[h] = qn
        qc = jnp.concatenate([qa * tabs[0] - qb * tabs[1], qb * tabs[2] + qa * tabs[3]], 0).astype(BF)
        qc_s[h] = qc
        sum_e = jnp.zeros((8, T), F32)
        sum_ep = jnp.zeros((8, T), F32)
        for s0 in range(0, T, HD):
            scores = nn(kall[g, T + s0 : T + s0 + HD], qc)
            prob = nt(vall[g, T + s0 : T + s0 + HD], cot)
            e = jnp.exp2(scores - SHIFT)
            if s0 == 0:
                e = jnp.concatenate([jnp.where(tri, e[:, :HD], 0.0), e[:, HD:]], 1)
            else:
                e = jnp.concatenate([jnp.zeros((HD, HD), F32), jnp.where(tri, e[:, HD:], 0.0)], 1)
            er_s[h, s0 : s0 + HD] = e
            pr_s[h, s0 : s0 + HD] = prob
            sum_e = sum_e + jnp.sum(e.reshape(HD // 8, 8, T), 0)
            sum_ep = sum_ep + jnp.sum((e * prob).reshape(HD // 8, 8, T), 0)
        se_s[h] = sum_e
        sp_s[h] = sum_ep

    steps = KVH * GW // UNROLL
    per = GW // UNROLL

    def when(i, at):
        return pl.when(i == at * per - 1)

    def first_parts(i, _):
        g = lax.div(i, per)

        @pl.when(lax.rem(i, per) == 0)
        def _():
            in_copy(0, g).wait()
            in_copy(1, g).wait()

        for j in range(UNROLL):
            first_part(g, i * UNROLL + j)

        @when(i, 1)
        def _():
            pl.semaphore_wait(barrier, 33)
            for g in range(KVH):
                for k in range(1, NX):
                    p1_copy(g, k, my_x).start()
                own_copy(g).start()
            for k in range(1, 8):
                rw_copy(k, me).start()

        return 0

    lax.fori_loop(0, steps, first_parts, 0)
    for g in range(KVH):
        bc1(g)

    for k in range(1, 8):
        rw_copy(k, behind(me, k, 8)).wait_recv()
    total = rw_buf[0]
    square = rw_buf[0] * rw_buf[0]
    for k in range(1, 8):
        total = total + rw_buf[k]
        square = square + rw_buf[k] * rw_buf[k]
    mean = total / 8
    spread = jnp.sqrt(jnp.maximum(square / 8 - mean * mean, 0.0))
    advantage = (rw_buf[me] - mean) / jnp.maximum(spread, 1.0)
    adv_s[...] = jnp.concatenate([advantage, advantage], 1)
    for g in range(KVH):
        bc2(g)

    def second_part(g, h, slot):
        cols = head_cols(h)
        cot = do_vm[:, cols]
        qc = qc_s[h]
        e_r, p_r, wb_r = e_s.at[slot], p_s.at[slot], wb_s.at[slot]
        sum_e = se_s[h]
        sum_ep = sp_s[h]
        for s0 in range(0, T, HD):
            block = slice(s0, s0 + HD)
            scores = nn(kall[g, block], qc)
            prob = nt(vall[g, block], cot)
            e = jnp.exp2(scores - SHIFT)
            e_r[block] = e
            p_r[block] = prob
            sum_e = sum_e + jnp.sum(e.reshape(HD // 8, 8, T), 0)
            sum_ep = sum_ep + jnp.sum((e * prob).reshape(HD // 8, 8, T), 0)
        inv = mask_s[0:1] / jnp.sum(sum_e, 0, keepdims=True)
        dots = jnp.sum(sum_ep, 0, keepdims=True) * inv
        se_s[h] = jnp.broadcast_to(inv, (8, T))
        sp_s[h] = jnp.broadcast_to(dots, (8, T))
        for s0 in range(0, T, HD):
            block = slice(s0, s0 + HD)
            w = e_r[block] * inv
            wb_r[block] = w.astype(BF)
            gb_s[h, block] = (w * (p_r[block] - dots)).astype(BF)
        dva[...] += nn(wb_r[...], cot)
        dkp[...] += nt(gb_s[h, 0:T], qc)

    def second_parts(i, _):
        g = lax.div(i, per)

        @pl.when(lax.rem(i, per) == 0)
        def _():
            bc3(g)
            dkp[...] = jnp.zeros_like(dkp)
            dva[...] = jnp.zeros_like(dva)

        for j in range(UNROLL):
            second_part(g, i * UNROLL + j, j)

        @pl.when(lax.rem(i, per) == per - 1)
        def _():
            rd1(g)

        @when(i, 3)
        def _():
            rd2(0)

        @when(i, 4)
        def _():
            rd2(1)

        return 0

    lax.fori_loop(0, steps, second_parts, 0)

    def third_part(g, h):
        cols = head_cols(h)
        inv = se_s[h, 0:1]
        dots = sp_s[h, 0:1]
        for s0 in range(0, T, HD):
            w = er_s[h, s0 : s0 + HD] * inv
            wr_s[h, s0 : s0 + HD] = w.astype(BF)
            gb_s[h, T + s0 : T + s0 + HD] = (w * (pr_s[h, s0 : s0 + HD] - dots)).astype(BF)
        dkr[...] += nt(gb_s[h, T : 2 * T], qc_s[h])
        dt = nn(kt_s[g], gb_s[h])
        da, db = dt[:64], dt[64:]
        va = da * tabs[0] + db * tabs[3]
        vb = db * tabs[2] - da * tabs[1]
        qa, qb = qn_s[h, 0:64], qn_s[h, 64:HD]
        pa, pb = va * qa, vb * qb
        gacc[0:64] += pa
        gacc[64:HD] += pb
        m = (jnp.sum(pa, 0, keepdims=True) + jnp.sum(pb, 0, keepdims=True)) * (1.0 / HD)
        r = r_s[h, 0:1] * (adv_s[0:1] * LN2)
        dx = jnp.concatenate([(va - qa * m) * r, (vb - qb * m) * r], 0).astype(BF)
        q_vm[:, cols] = dx.T

    def key_grads(g):
        dk = dkr[...] * LN2
        u = dk * nat_ref[0] - pltpu.roll(dk, HD // 2, 1) * nat_ref[1]
        kn = kn_s[g]
        gks[0:1] += jnp.sum(u * kn, 0, keepdims=True)
        v = u * gk
        m = jnp.mean(v * kn, -1, keepdims=True)
        dkv_vm[:, 0, head_cols(g)] = (rk_s[g] * adv_s[0:1, 0:HD] * (v - kn * m)).astype(BF)

    def third_parts(i, _):
        g = lax.div(i, per)

        @pl.when(lax.rem(i, per) == 0)
        def _():
            dkr[...] = jnp.zeros_like(dkr)

        for j in range(UNROLL):
            third_part(g, i * UNROLL + j)

        @pl.when(lax.rem(i, per) == per - 1)
        def _():
            key_grads(g)
            out_copy(g).start()

        @when(i, 1)
        def _():
            rd2(2)
            rd3(0)

        @when(i, 2)
        def _():
            rd2(3)
            rd3(1)

        @when(i, 3)
        def _():
            rd3(2)
            rd4(0)

        return 0

    lax.fori_loop(0, steps, third_parts, 0)
    last = KVH - 1

    def stage(buf, mine, peer, ss, rs):
        def copy(k, slot):
            return remote(buf.at[mine], buf.at[slot], ss.at[k], rs.at[k], peer(k))

        def start():
            for k in range(1, 16):
                copy(k, mine).start()

        def finish():
            for k in range(1, 16):
                copy(k, behind(mine, k, 16)).wait_recv()
            out = buf[0]
            for k in range(1, 16):
                out = out + buf[k]
            return out

        def drain():
            for k in range(1, 16):
                copy(k, mine).wait_send()

        return start, finish, drain

    ga_start, ga_finish, ga_drain = stage(ga_buf, my_a, a_peer, ga_s, ga_r)
    gb_start, gb_finish, gb_drain = stage(gb_buf, my_b, b_peer, gb2_s, gb2_r)

    gq = jnp.broadcast_to(jnp.sum(gacc[...], 1, keepdims=True), (HD, HD)).T * LN2 / gain_ref[0:1, :]
    ga_buf[my_a] = jnp.concatenate([gq[0:1], gks[0:1], jnp.zeros((6, HD), F32)], 0) * adv_s[:, 0:HD]
    ga_start()

    def value_grads(g, _):
        total = jnp.zeros((T, HD), F32)
        for j in range(GW):
            h = g * GW + j
            total = total + nn(wr_s[h], do_vm[:, head_cols(h)])
        dkv_vm[:, 1, head_cols(g)] = (total * adv_s[0:1, 0:HD]).astype(BF)
        return 0

    rd3(last)
    lax.fori_loop(0, KVH, value_grads, 0)
    rd4(1)
    gb_buf[my_b] = ga_finish()
    gb_start()
    dkv_copy = pltpu.make_async_copy(dkv_vm, dkv_hbm, out_sem.at[4])
    dkv_copy.start()
    rd4(2)
    for k in range(1, 8):
        rw_copy(k, me).wait_send()
    ga_drain()
    for g in range(KVH):
        bz_copy(g, my_z).wait_send()
        rz_copy(g).wait_send()
        for k in range(1, NX):
            p1_copy(g, k, my_x).wait_send()
            ag_copy(g, k, my_x).wait_send()
            rs_copy(g, k, my_x).wait_send()
        out_copy(g).wait()
    rd4(last)
    dpx_copy = pltpu.make_async_copy(dpx_vm, dpx_hbm, out_sem.at[5])
    dpx_copy.start()
    dg_ref[...] = gb_finish()[0:2] * (1.0 / 256)
    gb_drain()
    for g in range(KVH):
        for k in range(1, NX):
            fg_copy(g, k, my_x).wait_send()
    dkv_copy.wait()
    dpx_copy.wait()


def body(queries, resp_kv, prefix_kv, norm_gains, dout, lengths, rewards, owner):
    natural, transposed = tables()
    anywhere = pl.BlockSpec(memory_space=pl.ANY)
    vmem = pl.BlockSpec(memory_space=pltpu.VMEM)
    dma = pltpu.SemaphoreType.DMA
    heads = KVH * GW
    out = pl.pallas_call(
        kernel,
        out_shape=[
            jax.ShapeDtypeStruct((T, 4096), BF),
            jax.ShapeDtypeStruct((T, 2, 512), BF),
            jax.ShapeDtypeStruct((T, 2, 512), BF),
            jax.ShapeDtypeStruct((2, HD), F32),
        ],
        in_specs=[anywhere] * 10,
        out_specs=[anywhere, anywhere, anywhere, vmem],
        scratch_shapes=[
            pltpu.VMEM((2, HD), F32),
            pltpu.VMEM((2, T, HD), F32),
            pltpu.VMEM((2, HD // 2, T), F32),
            pltpu.SMEM((1, 1), jnp.int32),
            pltpu.SMEM((1, 1), jnp.int32),
            pltpu.SMEM((1,), jnp.int32),
            pltpu.VMEM((T, 4096), BF),
            pltpu.VMEM((T, 4096), BF),
            pltpu.VMEM((T, 2, 512), BF),
            pltpu.VMEM((T, 2, 512), BF),
            pltpu.VMEM((T, 2, 512), BF),
            pltpu.VMEM((heads, HD, T), F32),
            pltpu.VMEM((heads, HD, T), BF),
            pltpu.VMEM((heads, 8, T), F32),
            pltpu.VMEM((heads, T, T), F32),
            pltpu.VMEM((heads, T, T), F32),
            pltpu.VMEM((heads, 8, T), F32),
            pltpu.VMEM((heads, 8, T), F32),
            pltpu.VMEM((heads, T, T), BF),
            pltpu.VMEM((KVH, 2 * T, HD), BF),
            pltpu.VMEM((KVH, 2 * T, HD), BF),
            pltpu.VMEM((KVH, HD, 2 * T), BF),
            pltpu.VMEM((KVH, T, HD), F32),
            pltpu.VMEM((KVH, T, HD), F32),
            pltpu.VMEM((4, HD // 2, T), F32),
            pltpu.VMEM((8, T), F32),
            pltpu.VMEM((8, T), F32),
            pltpu.VMEM((T, HD), F32),
            pltpu.VMEM((T, HD), F32),
            pltpu.VMEM((T, HD), F32),
            pltpu.VMEM((HD, T), F32),
            pltpu.VMEM((8, HD), F32),
            pltpu.VMEM((UNROLL, T, T), F32),
            pltpu.VMEM((UNROLL, T, T), F32),
            pltpu.VMEM((UNROLL, T, T), BF),
            pltpu.VMEM((heads, 2 * T, T), BF),
            [pltpu.VMEM((NX, CH, 2, HD), BF)] * KVH,
            [pltpu.VMEM((2, CH, 2, HD), BF)] * KVH,
            pltpu.VMEM((KVH, T, 2, HD), BF),
            pltpu.VMEM((KVH, T, 2 * HD), BF),
            pltpu.VMEM((KVH, NX, CH, 2 * HD), BF),
            pltpu.VMEM((KVH, CH, 2 * HD), BF),
            pltpu.VMEM((KVH, CH, 2 * HD), BF),
            pltpu.VMEM((KVH, CH, 2 * HD), F32),
            pltpu.VMEM((KVH, T, 2 * HD), BF),
            pltpu.VMEM((8, 8, HD), F32),
            pltpu.VMEM((16, 8, HD), F32),
            pltpu.VMEM((16, 8, HD), F32),
            dma((2, KVH)),
            dma((7,)),
            dma((6,)),
            dma((KVH,)),
            dma((KVH, NX)),
            dma((KVH, NX)),
            dma((KVH,)),
            dma((KVH,)),
            dma((KVH, NX)),
            dma((KVH, NX)),
            dma((KVH, NX)),
            dma((KVH, NX)),
            dma((KVH,)),
            dma((KVH,)),
            dma((KVH, NX)),
            dma((KVH, NX)),
            dma((8,)),
            dma((8,)),
            dma((16,)),
            dma((16,)),
            dma((16,)),
            dma((16,)),
        ],
        compiler_params=pltpu.CompilerParams(
            collective_id=0, has_side_effects=True, vmem_limit_bytes=56 << 20
        ),
    )(
        queries[0, 0], resp_kv[0, 0], prefix_kv[0, 0], norm_gains, dout[0, 0],
        lengths, rewards, owner, natural, transposed,
    )
    return (out[0][None, None], out[1][None, None], out[2][None, None], out[3])


def solution(mesh):
    return jax.shard_map(
        body,
        mesh=mesh,
        in_specs=(
            P("prompts", "group", None, None),
            P("prompts", "group", None, None, None),
            P("prompts", "group", None, None, None),
            P(),
            P("prompts", "group", None, None),
            P("prompts", "group"),
            P("prompts", "group"),
            P("prompts"),
        ),
        out_specs=(
            P("prompts", "group", None, None),
            P("prompts", "group", None, None, None),
            P("prompts", "group", None, None, None),
            P(),
        ),
        check_vma=False,
    )
```

time: 90.2 us -> 73.4 us (0.81)
  Pallas kernels: 79.3 us -> 65.3 us
  local copies, waits for them, and re-layouts: 8.08 us -> 5.38 us
    pallas_call x1, Pallas kernels: 79.3 us -> 65.3 us  [body(): pl.pallas_call(kernel, out_shape=[jax.ShapeDtypeStruct((T, 4096), BF), ja...]
    unnamed x14 -> x10, local copies, waits for them, and re-layouts: 8.08 us -> 5.38 us
where the time goes in v2:
time: 73.4 us; the launch traced here: 73.3 us
  Pallas kernels  65.3 us (89%)
  local copies, waits for them, and re-layouts  5.38 us (7%)
  between operations  2.6 us (4%)
    pallas_call x1, Pallas kernels, body(): pl.pallas_call(kernel, out_shape=[jax.ShapeDtypeStruct((T, 4096), BF), ja...  65.3 us
    unnamed x10, local copies, waits for them, and re-layouts  5.38 us

profile of v2, /device:TPU:1, one launch (start us, length us, event | category | flops | bytes accessed | tf_op | source)
XLA Modules:
  0.0 73.3 jit_solution(3583438392551960859)
XLA Ops:
  2.6 65.3 %shard_map.129 = (bf16[256,4096]{1,0:T(8,128)(2,1)}, bf16[256,2,512]{2,1,0:T(2,128)(2,1)}, bf16[256,2,512]{2,1,0:T(2,128)(2,1)}, f32[2,128]{1,0:T(2,128)}) custom-call(bf16[256,4096]{1,0:T(8,128)(2,1)} %bitcast.7, bf16[256,2,512]{2,1,0:T(2,128)(2,1)} %bitcast.12, bf16[256,2,512]{2,1,0:T(2,128)(2,1)} %bitcast.13, f32[2,128]{1,0:T(2,128)} %gain_hbm.1, ...), custom_call_target="tpu_custom_call" | custom-call | tf_op jit(solution)/shard_map/pallas_call | solution.py:509
  67.9 0.0 copy-start.1
  67.9 0.0 copy-start
  67.9 3.2 %copy.21 = bf16[1,1,256,4096]{3,2,1,0:T(8,128)(2,1)} copy(bf16[1,1,256,4096]{3,2,1,0:T(8,128)(2,1)} %bitcast.9) | data formatting | bytes 4194304
  71.1 0.0 copy-done.1
  71.1 0.0 copy-start.2
  71.1 0.8 %copy.22 = bf16[1,1,256,2,512]{4,3,2,1,0:T(2,128)(2,1)} copy(bf16[1,1,256,2,512]{4,3,2,1,0:T(2,128)(2,1)S(1)} %bitcast.11) | data formatting | bytes 1048576
  71.9 0.0 copy-done
  71.9 0.8 %copy.23 = bf16[1,1,256,2,512]{4,3,2,1,0:T(2,128)(2,1)} copy(bf16[1,1,256,2,512]{4,3,2,1,0:T(2,128)(2,1)S(1)} %bitcast.10) | data formatting | bytes 1048576
  72.7 0.0 copy-done.2
  72.7 0.6 copy.24
Async XLA Ops:
  67.9 3.2 %copy-start.1 = (bf16[256,2,512]{2,1,0:T(2,128)(2,1)S(1)}, bf16[256,2,512]{2,1,0:T(2,128)(2,1)}, u32[]{:S(2)}) copy-start(bf16[256,2,512]{2,1,0:T(2,128)(2,1)} %get-tuple-element.9) | copy-start | bytes 1572868
  67.9 4.0 %copy-start = (bf16[256,2,512]{2,1,0:T(2,128)(2,1)S(1)}, bf16[256,2,512]{2,1,0:T(2,128)(2,1)}, u32[]{:S(2)}) copy-start(bf16[256,2,512]{2,1,0:T(2,128)(2,1)} %get-tuple-element.10) | copy-start | bytes 1572868
  71.1 1.6 %copy-start.2 = (f32[2,128]{1,0:T(2,128)S(1)}, f32[2,128]{1,0:T(2,128)}, u32[]{:S(2)}) copy-start(f32[2,128]{1,0:T(2,128)} %get-tuple-element.19) | copy-start | bytes 3076

commit v3 on v2

--- a/solution.py
+++ b/solution.py
@@ -20,7 +20,6 @@
 LOG2E = 1.4426950408889634
 LN2 = 0.6931471805599453
 SHIFT = 40.0
-UNROLL = 4
 F32 = jnp.float32
 BF = jnp.bfloat16
 MESH = pl.DeviceIdType.MESH
@@ -52,7 +51,7 @@
     e_s, p_s, wb_s, gb_s,
     a_buf, b_buf, c_buf, r_buf, rr_buf, t_buf, tt_buf, tf_buf, ff_buf,
     rw_buf, ga_buf, gb_buf,
-    in_sem, small_sem, out_sem, own_sem,
+    in_sem, small_sem, out_sem, own_sem, px_sem,
     p1_s, p1_r, bz_s, bz_r, ag_s, ag_r, rs_s, rs_r, rz_s, rz_r, fg_s, fg_r,
     rw_s, rw_r, ga_s, ga_r, gb2_s, gb2_r,
 ):
@@ -91,8 +90,9 @@
         pl.semaphore_signal(barrier, inc=1, device_id=dev, device_id_type=MESH)
 
     barrier = pltpu.get_barrier_semaphore()
+    for k in range(15, 0, -1):
+        greet(b_peer(k))
     for k in range(1, 16):
-        greet(b_peer(k))
         greet(a_peer(k))
     for k in range(1, NX):
         greet({"group": (1 - my_z) * NX + lax.rem(my_x + k, NX), "prompts": pr})
@@ -113,9 +113,23 @@
     def out_copy(g):
         return pltpu.make_async_copy(q_vm.at[:, wide(g)], dq_hbm.at[:, wide(g)], out_sem.at[g])
 
+    def head_cols(g):
+        return pl.ds(pl.multiple_of(g * HD, HD), HD)
+
+    def rows(x):
+        return pl.ds(pl.multiple_of(x * CH, CH), CH)
+
+    def p1_copy(g, k, slot):
+        src = px_hbm.at[rows(lax.rem(my_x + k, NX)), :, head_cols(g)]
+        return remote(src, a_buf[g].at[slot], p1_s.at[g, k], p1_r.at[g, k], x_peer(k))
+
+    def own_copy(g):
+        return pltpu.make_async_copy(px_hbm.at[rows(my_x), :, head_cols(g)], a_buf[g].at[my_x], own_sem.at[g])
+
     for copy in small_copies:
         copy.start()
     for g in range(KVH):
+        own_copy(g).start()
         in_copy(0, g).start()
         in_copy(1, g).start()
     for copy in small_copies:
@@ -137,21 +151,9 @@
     owner = own_ref[0]
     owner_x, owner_z = lax.rem(owner, NX), lax.div(owner, NX)
 
-    def head_cols(g):
-        return pl.ds(pl.multiple_of(g * HD, HD), HD)
-
-    def rows(x):
-        return pl.ds(pl.multiple_of(x * CH, CH), CH)
-
     def rw_copy(k, slot):
         return remote(rw_buf.at[me], rw_buf.at[slot], rw_s.at[k], rw_r.at[k], g_peer(k))
 
-    def p1_copy(g, k, slot):
-        src = px_hbm.at[rows(lax.rem(my_x + k, NX)), :, head_cols(g)]
-        return remote(src, a_buf[g].at[slot], p1_s.at[g, k], p1_r.at[g, k], x_peer(k))
-
-    def own_copy(g):
-        return pltpu.make_async_copy(px_hbm.at[rows(my_x), :, head_cols(g)], a_buf[g].at[my_x], own_sem.at[g])
 
     def bz_copy(g, slot):
         return remote(b_buf[g].at[my_z], b_buf[g].at[slot], bz_s.at[g], bz_r.at[g], z_peer)
@@ -213,6 +215,10 @@
         for k in range(1, NX):
             fg_copy(g, k, my_x).start()
 
+    def dpx_copy(g):
+        cols = head_cols(g)
+        return pltpu.make_async_copy(dpx_vm.at[:, :, cols], dpx_hbm.at[:, :, cols], px_sem.at[g])
+
     def rd4(g):
         for k in range(1, NX):
             fg_copy(g, k, behind(my_x, k, NX)).wait_recv()
@@ -220,6 +226,7 @@
         cols = head_cols(g)
         dpx_vm[:, 0, cols] = jnp.where(mine, ff_buf[g, :, 0:HD], jnp.zeros((T, HD), BF))
         dpx_vm[:, 1, cols] = jnp.where(mine, ff_buf[g, :, HD:], jnp.zeros((T, HD), BF))
+        dpx_copy(g).start()
 
     def key_prep(g, _):
         cols = head_cols(g)
@@ -235,7 +242,21 @@
 
     lax.fori_loop(0, KVH, key_prep, 0)
 
-    def first_part(g, h):
+    pl.semaphore_wait(barrier, 33)
+    for g in range(KVH):
+        for k in range(1, NX):
+            p1_copy(g, k, my_x).start()
+    for k in range(1, 8):
+        rw_copy(k, me).start()
+
+    def lanes(j):
+        return slice(j * T, j * T + T)
+
+    def cots(g):
+        return jnp.concatenate([do_vm[:, head_cols(g * GW + j)] for j in range(GW)], 0)
+
+    def first_part(g, j):
+        h = g * GW + j
         cols = head_cols(h)
         cot = do_vm[:, cols]
         x = q_vm[:, cols].T.astype(F32)
@@ -245,7 +266,7 @@
         r_s[h] = jnp.broadcast_to(r, (8, T))
         qn_s[h] = qn
         qc = jnp.concatenate([qa * tabs[0] - qb * tabs[1], qb * tabs[2] + qa * tabs[3]], 0).astype(BF)
-        qc_s[h] = qc
+        qc_s[g, :, lanes(j)] = qc
         sum_e = jnp.zeros((8, T), F32)
         sum_ep = jnp.zeros((8, T), F32)
         for s0 in range(0, T, HD):
@@ -263,38 +284,28 @@
         se_s[h] = sum_e
         sp_s[h] = sum_ep
 
-    steps = KVH * GW // UNROLL
-    per = GW // UNROLL
-
-    def when(i, at):
-        return pl.when(i == at * per - 1)
-
-    def first_parts(i, _):
-        g = lax.div(i, per)
-
-        @pl.when(lax.rem(i, per) == 0)
+    def first_parts(g, _):
+        in_copy(0, g).wait()
+        in_copy(1, g).wait()
+        for j in range(GW):
+            first_part(g, j)
+
+        @pl.when(g == 2)
         def _():
-            in_copy(0, g).wait()
-            in_copy(1, g).wait()
-
-        for j in range(UNROLL):
-            first_part(g, i * UNROLL + j)
-
-        @when(i, 1)
+            bc1(0)
+            bc1(1)
+
+        @pl.when(g == 3)
         def _():
-            pl.semaphore_wait(barrier, 33)
-            for g in range(KVH):
-                for k in range(1, NX):
-                    p1_copy(g, k, my_x).start()
-                own_copy(g).start()
-            for k in range(1, 8):
-                rw_copy(k, me).start()
+            bc1(2)
+            bc1(3)
 
         return 0
 
-    lax.fori_loop(0, steps, first_parts, 0)
+    lax.fori_loop(0, KVH, first_parts, 0)
+
     for g in range(KVH):
-        bc1(g)
+        bc2(g)
 
     for k in range(1, 8):
         rw_copy(k, behind(me, k, 8)).wait_recv()
@@ -307,14 +318,13 @@
     spread = jnp.sqrt(jnp.maximum(square / 8 - mean * mean, 0.0))
     advantage = (rw_buf[me] - mean) / jnp.maximum(spread, 1.0)
     adv_s[...] = jnp.concatenate([advantage, advantage], 1)
-    for g in range(KVH):
-        bc2(g)
-
-    def second_part(g, h, slot):
+
+    def second_part(g, j):
+        h = g * GW + j
         cols = head_cols(h)
         cot = do_vm[:, cols]
-        qc = qc_s[h]
-        e_r, p_r, wb_r = e_s.at[slot], p_s.at[slot], wb_s.at[slot]
+        qc = qc_s[g, :, lanes(j)]
+        e_r, p_r = e_s.at[j], p_s.at[j]
         sum_e = se_s[h]
         sum_ep = sp_s[h]
         for s0 in range(0, T, HD):
@@ -333,49 +343,35 @@
         for s0 in range(0, T, HD):
             block = slice(s0, s0 + HD)
             w = e_r[block] * inv
-            wb_r[block] = w.astype(BF)
-            gb_s[h, block] = (w * (p_r[block] - dots)).astype(BF)
-        dva[...] += nn(wb_r[...], cot)
-        dkp[...] += nt(gb_s[h, 0:T], qc)
-
-    def second_parts(i, _):
-        g = lax.div(i, per)
-
-        @pl.when(lax.rem(i, per) == 0)
-        def _():
-            bc3(g)
-            dkp[...] = jnp.zeros_like(dkp)
-            dva[...] = jnp.zeros_like(dva)
-
-        for j in range(UNROLL):
-            second_part(g, i * UNROLL + j, j)
-
-        @pl.when(lax.rem(i, per) == per - 1)
-        def _():
-            rd1(g)
-
-        @when(i, 3)
+            wb_s[block, lanes(j)] = w.astype(BF)
+            gb_s[g, block, lanes(j)] = (w * (p_r[block] - dots)).astype(BF)
+
+    def second_parts(g, _):
+        bc3(g)
+        for j in range(GW):
+            second_part(g, j)
+        dva[...] = nn(wb_s[...], cots(g))
+        dkp[...] = nt(gb_s[g, 0:T], qc_s[g])
+        rd1(g)
+
+        @pl.when(g == 3)
         def _():
             rd2(0)
 
-        @when(i, 4)
-        def _():
-            rd2(1)
-
         return 0
 
-    lax.fori_loop(0, steps, second_parts, 0)
-
-    def third_part(g, h):
+    lax.fori_loop(0, KVH, second_parts, 0)
+
+    def third_part(g, j):
+        h = g * GW + j
         cols = head_cols(h)
         inv = se_s[h, 0:1]
         dots = sp_s[h, 0:1]
         for s0 in range(0, T, HD):
             w = er_s[h, s0 : s0 + HD] * inv
-            wr_s[h, s0 : s0 + HD] = w.astype(BF)
-            gb_s[h, T + s0 : T + s0 + HD] = (w * (pr_s[h, s0 : s0 + HD] - dots)).astype(BF)
-        dkr[...] += nt(gb_s[h, T : 2 * T], qc_s[h])
-        dt = nn(kt_s[g], gb_s[h])
+            wr_s[g, s0 : s0 + HD, lanes(j)] = w.astype(BF)
+            gb_s[g, T + s0 : T + s0 + HD, lanes(j)] = (w * (pr_s[h, s0 : s0 + HD] - dots)).astype(BF)
+        dt = nn(kt_s[g], gb_s[g, :, lanes(j)])
         da, db = dt[:64], dt[64:]
         va = da * tabs[0] + db * tabs[3]
         vb = db * tabs[2] - da * tabs[1]
@@ -397,39 +393,28 @@
         m = jnp.mean(v * kn, -1, keepdims=True)
         dkv_vm[:, 0, head_cols(g)] = (rk_s[g] * adv_s[0:1, 0:HD] * (v - kn * m)).astype(BF)
 
-    def third_parts(i, _):
-        g = lax.div(i, per)
-
-        @pl.when(lax.rem(i, per) == 0)
+    def third_parts(g, _):
+        for j in range(GW):
+            third_part(g, j)
+        dkr[...] = nt(gb_s[g, T : 2 * T], qc_s[g])
+        key_grads(g)
+        out_copy(g).start()
+
+        @pl.when(g == 0)
         def _():
-            dkr[...] = jnp.zeros_like(dkr)
-
-        for j in range(UNROLL):
-            third_part(g, i * UNROLL + j)
-
-        @pl.when(lax.rem(i, per) == per - 1)
-        def _():
-            key_grads(g)
-            out_copy(g).start()
-
-        @when(i, 1)
+            rd2(1)
+
+        @pl.when(g == 1)
         def _():
             rd2(2)
-            rd3(0)
-
-        @when(i, 2)
+
+        @pl.when(g == 2)
         def _():
             rd2(3)
-            rd3(1)
-
-        @when(i, 3)
-        def _():
-            rd3(2)
-            rd4(0)
 
         return 0
 
-    lax.fori_loop(0, steps, third_parts, 0)
+    lax.fori_loop(0, KVH, third_parts, 0)
     last = KVH - 1
 
     def stage(buf, mine, peer, ss, rs):
@@ -460,22 +445,23 @@
     gq = jnp.broadcast_to(jnp.sum(gacc[...], 1, keepdims=True), (HD, HD)).T * LN2 / gain_ref[0:1, :]
     ga_buf[my_a] = jnp.concatenate([gq[0:1], gks[0:1], jnp.zeros((6, HD), F32)], 0) * adv_s[:, 0:HD]
     ga_start()
+    rd3(0)
 
     def value_grads(g, _):
-        total = jnp.zeros((T, HD), F32)
-        for j in range(GW):
-            h = g * GW + j
-            total = total + nn(wr_s[h], do_vm[:, head_cols(h)])
+        total = nn(wr_s[g], cots(g))
         dkv_vm[:, 1, head_cols(g)] = (total * adv_s[0:1, 0:HD]).astype(BF)
         return 0
 
+    lax.fori_loop(0, KVH, value_grads, 0)
+    dkv_copy = pltpu.make_async_copy(dkv_vm, dkv_hbm, out_sem.at[4])
+    dkv_copy.start()
+    rd3(1)
+    rd3(2)
     rd3(last)
-    lax.fori_loop(0, KVH, value_grads, 0)
-    rd4(1)
     gb_buf[my_b] = ga_finish()
     gb_start()
-    dkv_copy = pltpu.make_async_copy(dkv_vm, dkv_hbm, out_sem.at[4])
-    dkv_copy.start()
+    rd4(0)
+    rd4(1)
     rd4(2)
     for k in range(1, 8):
         rw_copy(k, me).wait_send()
@@ -488,16 +474,28 @@
             ag_copy(g, k, my_x).wait_send()
             rs_copy(g, k, my_x).wait_send()
         out_copy(g).wait()
+    dkv_copy.wait()
     rd4(last)
-    dpx_copy = pltpu.make_async_copy(dpx_vm, dpx_hbm, out_sem.at[5])
-    dpx_copy.start()
     dg_ref[...] = gb_finish()[0:2] * (1.0 / 256)
     gb_drain()
     for g in range(KVH):
         for k in range(1, NX):
             fg_copy(g, k, my_x).wait_send()
-    dkv_copy.wait()
-    dpx_copy.wait()
+        dpx_copy(g).wait()
+
+
+def finish(*refs):
+    sources, results, held, in_sem, out_sem = refs[:4], refs[4:8], refs[8:12], refs[12], refs[13]
+    parts = [(0, pl.ds(i * 64, 64)) for i in range(4)] + [(1, pl.ds(0, T)), (2, pl.ds(0, T)), (3, pl.ds(0, 2))]
+    arrive = [pltpu.make_async_copy(sources[a].at[p], held[a].at[p], in_sem.at[i]) for i, (a, p) in enumerate(parts)]
+    leave = [pltpu.make_async_copy(held[a].at[p], results[a].at[p], out_sem.at[i]) for i, (a, p) in enumerate(parts)]
+    for copy in arrive:
+        copy.start()
+    for came, goes in zip(arrive, leave):
+        came.wait()
+        goes.start()
+    for copy in leave:
+        copy.wait()
 
 
 def body(queries, resp_kv, prefix_kv, norm_gains, dout, lengths, rewards, owner):
@@ -506,14 +504,15 @@
     vmem = pl.BlockSpec(memory_space=pltpu.VMEM)
     dma = pltpu.SemaphoreType.DMA
     heads = KVH * GW
+    shapes = [
+        jax.ShapeDtypeStruct((T, 4096), BF),
+        jax.ShapeDtypeStruct((T, 2, 512), BF),
+        jax.ShapeDtypeStruct((T, 2, 512), BF),
+        jax.ShapeDtypeStruct((2, HD), F32),
+    ]
     out = pl.pallas_call(
         kernel,
-        out_shape=[
-            jax.ShapeDtypeStruct((T, 4096), BF),
-            jax.ShapeDtypeStruct((T, 2, 512), BF),
-            jax.ShapeDtypeStruct((T, 2, 512), BF),
-            jax.ShapeDtypeStruct((2, HD), F32),
-        ],
+        out_shape=shapes,
         in_specs=[anywhere] * 10,
         out_specs=[anywhere, anywhere, anywhere, vmem],
         scratch_shapes=[
@@ -529,13 +528,13 @@
             pltpu.VMEM((T, 2, 512), BF),
             pltpu.VMEM((T, 2, 512), BF),
             pltpu.VMEM((heads, HD, T), F32),
-            pltpu.VMEM((heads, HD, T), BF),
+            pltpu.VMEM((KVH, HD, GW * T), BF),
             pltpu.VMEM((heads, 8, T), F32),
             pltpu.VMEM((heads, T, T), F32),
             pltpu.VMEM((heads, T, T), F32),
             pltpu.VMEM((heads, 8, T), F32),
             pltpu.VMEM((heads, 8, T), F32),
-            pltpu.VMEM((heads, T, T), BF),
+            pltpu.VMEM((KVH, T, GW * T), BF),
             pltpu.VMEM((KVH, 2 * T, HD), BF),
             pltpu.VMEM((KVH, 2 * T, HD), BF),
             pltpu.VMEM((KVH, HD, 2 * T), BF),
@@ -549,10 +548,10 @@
             pltpu.VMEM((T, HD), F32),
             pltpu.VMEM((HD, T), F32),
             pltpu.VMEM((8, HD), F32),
-            pltpu.VMEM((UNROLL, T, T), F32),
-            pltpu.VMEM((UNROLL, T, T), F32),
-            pltpu.VMEM((UNROLL, T, T), BF),
-            pltpu.VMEM((heads, 2 * T, T), BF),
+            pltpu.VMEM((GW, T, T), F32),
+            pltpu.VMEM((GW, T, T), F32),
+            pltpu.VMEM((T, GW * T), BF),
+            pltpu.VMEM((KVH, 2 * T, GW * T), BF),
             [pltpu.VMEM((NX, CH, 2, HD), BF)] * KVH,
             [pltpu.VMEM((2, CH, 2, HD), BF)] * KVH,
             pltpu.VMEM((KVH, T, 2, HD), BF),
@@ -569,6 +568,7 @@
             dma((7,)),
             dma((6,)),
             dma((KVH,)),
+            dma((KVH,)),
             dma((KVH, NX)),
             dma((KVH, NX)),
             dma((KVH,)),
@@ -595,6 +595,14 @@
         queries[0, 0], resp_kv[0, 0], prefix_kv[0, 0], norm_gains, dout[0, 0],
         lengths, rewards, owner, natural, transposed,
     )
+    out = pl.pallas_call(
+        finish,
+        out_shape=shapes,
+        in_specs=[anywhere] * 4,
+        out_specs=[anywhere] * 4,
+        scratch_shapes=[pltpu.VMEM(a.shape, a.dtype) for a in shapes] + [dma((7,)), dma((7,))],
+        compiler_params=pltpu.CompilerParams(vmem_limit_bytes=56 << 20),
+    )(*out)
     return (out[0][None, None], out[1][None, None], out[2][None, None], out[3])
 
 

time: 73.4 us -> 60 us (0.82)
  Pallas kernels: 65.3 us -> 57.3 us
  local copies, waits for them, and re-layouts: 5.38 us -> 0 us
    pallas_call x1 -> x2, Pallas kernels: 65.3 us -> 57.3 us  [the longest x1 54.5 us: body(): pl.pallas_call(kernel, out_shape=shapes, in_specs=[anywhere] * 10, out_sp...]
    unnamed x10 -> x0, local copies, waits for them, and re-layouts: 5.38 us -> none
where the time goes in v3:
time: 60 us; the launch traced here: 59.9 us
  Pallas kernels  57.3 us (96%)
  between operations  2.58 us (4%)
    pallas_call x1, Pallas kernels, body(): pl.pallas_call(kernel, out_shape=shapes, in_specs=[anywhere] * 10, out_sp...  54.5 us
    pallas_call x1, Pallas kernels, body(): pl.pallas_call(finish, out_shape=shapes, in_specs=[anywhere] * 4, out_spe...  2.82 us

profile of v3, /device:TPU:1, one launch (start us, length us, event | category | flops | bytes accessed | tf_op | source)
XLA Modules:
  0.0 59.9 jit_solution(9628090396202866803)
XLA Ops:
  2.6 54.5 %shard_map.129 = (bf16[256,4096]{1,0:T(8,128)(2,1)}, bf16[256,2,512]{2,1,0:T(2,128)(2,1)}, bf16[256,2,512]{2,1,0:T(2,128)(2,1)}, f32[2,128]{1,0:T(2,128)}) custom-call(bf16[256,4096]{1,0:T(8,128)(2,1)} %bitcast.7, bf16[256,2,512]{2,1,0:T(2,128)(2,1)} %bitcast.9, bf16[256,2,512]{2,1,0:T(2,128)(2,1)} %bitcast.10, f32[2,128]{1,0:T(2,128)} %gain_hbm.1, ...), custom_call_target="tpu_custom_call" | custom-call | tf_op jit(solution)/shard_map/pallas_call | solution.py:513
  57.1 2.8 %shard_map.130 = (bf16[256,4096]{1,0:T(8,128)(2,1)}, bf16[256,2,512]{2,1,0:T(2,128)(2,1)}, bf16[256,2,512]{2,1,0:T(2,128)(2,1)}, f32[2,128]{1,0:T(2,128)}) custom-call(bf16[256,4096]{1,0:T(8,128)(2,1)} %get-tuple-element.12.refs_0_, bf16[256,2,512]{2,1,0:T(2,128)(2,1)} %get-tuple-element.13.refs_1_, bf16[256,2,512]{2,1,0:T(2,128)(2,1)} %get-tuple-element.14.refs_2_, ...), custom_call_target="tpu_custom_call" | custom-call | tf_op jit(solution)/shard_map/pallas_call | solution.py:598

commit v4 on v3

--- a/solution.py
+++ b/solution.py
@@ -45,7 +45,7 @@
     q_hbm, kv_hbm, px_hbm, gain_hbm, do_hbm, len_hbm, rew_hbm, own_hbm, nat_hbm, tr_hbm,
     dq_hbm, dkv_hbm, dpx_hbm, dg_ref,
     gain_ref, nat_ref, tr_ref, len_ref, rew_ref, own_ref,
-    q_vm, do_vm, kv_vm, dkv_vm, dpx_vm,
+    q_vm, do_vm, kv_vm, px_vm, dkv_vm, dpx_vm,
     qn_s, qc_s, r_s, er_s, pr_s, se_s, sp_s, wr_s, kall, vall, kt_s, kn_s, rk_s, tabs, mask_s, adv_s,
     dkp, dkr, dva, gacc, gks,
     e_s, p_s, wb_s, gb_s,
@@ -120,16 +120,20 @@
         return pl.ds(pl.multiple_of(x * CH, CH), CH)
 
     def p1_copy(g, k, slot):
-        src = px_hbm.at[rows(lax.rem(my_x + k, NX)), :, head_cols(g)]
+        src = px_vm.at[g, rows(lax.rem(my_x + k, NX))]
         return remote(src, a_buf[g].at[slot], p1_s.at[g, k], p1_r.at[g, k], x_peer(k))
 
     def own_copy(g):
-        return pltpu.make_async_copy(px_hbm.at[rows(my_x), :, head_cols(g)], a_buf[g].at[my_x], own_sem.at[g])
-
+        return pltpu.make_async_copy(px_vm.at[g, rows(my_x)], a_buf[g].at[my_x], own_sem.at[g])
+
+    def px_copy(g):
+        return pltpu.make_async_copy(px_hbm.at[:, :, head_cols(g)], px_vm.at[g], px_sem.at[KVH + g])
+
+    for g in range(KVH):
+        px_copy(g).start()
     for copy in small_copies:
         copy.start()
     for g in range(KVH):
-        own_copy(g).start()
         in_copy(0, g).start()
         in_copy(1, g).start()
     for copy in small_copies:
@@ -171,7 +175,7 @@
     def bc2(g):
         bz_copy(g, 1 - my_z).wait_recv()
         c_buf[g, rows(my_x)] = b_buf[g][owner_z]
-        for k in range(1, NX):
+        for k in (2, 1, 3):
             ag_copy(g, k, my_x).start()
 
     def bc3(g):
@@ -195,7 +199,7 @@
         adv = adv_s[0:1, 0:HD]
         r_buf[g, :, 0:HD] = (dkp[...] * (adv * LN2)).astype(BF)
         r_buf[g, :, HD:] = (dva[...] * adv).astype(BF)
-        for k in range(1, NX):
+        for k in (2, 1, 3):
             rs_copy(g, k, my_x).start()
         tf_buf[g, :, 0:HD] = dkp[rows(my_x)] * (adv * LN2)
         tf_buf[g, :, HD:] = dva[rows(my_x)] * adv
@@ -212,7 +216,7 @@
     def rd3(g):
         rz_copy(g).wait_recv()
         ff_buf[g, rows(my_x)] = (tf_buf[g] + tt_buf[g].astype(F32)).astype(BF)
-        for k in range(1, NX):
+        for k in (2, 1, 3):
             fg_copy(g, k, my_x).start()
 
     def dpx_copy(g):
@@ -242,9 +246,12 @@
 
     lax.fori_loop(0, KVH, key_prep, 0)
 
+    for g in range(KVH):
+        px_copy(g).wait()
+        own_copy(g).start()
     pl.semaphore_wait(barrier, 33)
     for g in range(KVH):
-        for k in range(1, NX):
+        for k in (2, 1, 3):
             p1_copy(g, k, my_x).start()
     for k in range(1, 8):
         rw_copy(k, me).start()
@@ -375,14 +382,21 @@
         da, db = dt[:64], dt[64:]
         va = da * tabs[0] + db * tabs[3]
         vb = db * tabs[2] - da * tabs[1]
-        qa, qb = qn_s[h, 0:64], qn_s[h, 64:HD]
-        pa, pb = va * qa, vb * qb
-        gacc[0:64] += pa
-        gacc[64:HD] += pb
-        m = (jnp.sum(pa, 0, keepdims=True) + jnp.sum(pb, 0, keepdims=True)) * (1.0 / HD)
-        r = r_s[h, 0:1] * (adv_s[0:1] * LN2)
-        dx = jnp.concatenate([(va - qa * m) * r, (vb - qb * m) * r], 0).astype(BF)
-        q_vm[:, cols] = dx.T
+        er_s[h, 0:64] = va
+        er_s[h, 64:HD] = vb
+        return va * qn_s[h, 0:64], vb * qn_s[h, 64:HD]
+
+    def query_grads(g, _):
+        for j in range(GW):
+            h = g * GW + j
+            va, vb = er_s[h, 0:64], er_s[h, 64:HD]
+            qa, qb = qn_s[h, 0:64], qn_s[h, 64:HD]
+            m = jnp.sum(va * qa + vb * qb, 0, keepdims=True) * (1.0 / HD)
+            r = r_s[h, 0:1] * (adv_s[0:1] * LN2)
+            dx = jnp.concatenate([(va - qa * m) * r, (vb - qb * m) * r], 0).astype(BF)
+            q_vm[:, head_cols(h)] = dx.T
+        out_copy(g).start()
+        return 0
 
     def key_grads(g):
         dk = dkr[...] * LN2
@@ -394,11 +408,14 @@
         dkv_vm[:, 0, head_cols(g)] = (rk_s[g] * adv_s[0:1, 0:HD] * (v - kn * m)).astype(BF)
 
     def third_parts(g, _):
+        sum_a = sum_b = jnp.zeros((HD // 2, T), F32)
         for j in range(GW):
-            third_part(g, j)
+            pa, pb = third_part(g, j)
+            sum_a, sum_b = sum_a + pa, sum_b + pb
+        gacc[0:64] += sum_a
+        gacc[64:HD] += sum_b
         dkr[...] = nt(gb_s[g, T : 2 * T], qc_s[g])
         key_grads(g)
-        out_copy(g).start()
 
         @pl.when(g == 0)
         def _():
@@ -417,12 +434,12 @@
     lax.fori_loop(0, KVH, third_parts, 0)
     last = KVH - 1
 
-    def stage(buf, mine, peer, ss, rs):
+    def stage(buf, mine, peer, ss, rs, order):
         def copy(k, slot):
             return remote(buf.at[mine], buf.at[slot], ss.at[k], rs.at[k], peer(k))
 
         def start():
-            for k in range(1, 16):
+            for k in order:
                 copy(k, mine).start()
 
         def finish():
@@ -439,24 +456,29 @@
 
         return start, finish, drain
 
-    ga_start, ga_finish, ga_drain = stage(ga_buf, my_a, a_peer, ga_s, ga_r)
-    gb_start, gb_finish, gb_drain = stage(gb_buf, my_b, b_peer, gb2_s, gb2_r)
+    ga_start, ga_finish, ga_drain = stage(
+        ga_buf, my_a, a_peer, ga_s, ga_r, (10, 6, 9, 11, 7, 5, 14, 13, 2, 8, 3, 15, 1, 12, 4)
+    )
+    gb_start, gb_finish, gb_drain = stage(
+        gb_buf, my_b, b_peer, gb2_s, gb2_r, (8, 9, 7, 10, 6, 11, 5, 12, 4, 13, 3, 14, 2, 15, 1)
+    )
 
     gq = jnp.broadcast_to(jnp.sum(gacc[...], 1, keepdims=True), (HD, HD)).T * LN2 / gain_ref[0:1, :]
     ga_buf[my_a] = jnp.concatenate([gq[0:1], gks[0:1], jnp.zeros((6, HD), F32)], 0) * adv_s[:, 0:HD]
     ga_start()
     rd3(0)
+    lax.fori_loop(0, KVH, query_grads, 0)
 
     def value_grads(g, _):
         total = nn(wr_s[g], cots(g))
         dkv_vm[:, 1, head_cols(g)] = (total * adv_s[0:1, 0:HD]).astype(BF)
         return 0
 
+    rd3(1)
+    rd3(2)
     lax.fori_loop(0, KVH, value_grads, 0)
     dkv_copy = pltpu.make_async_copy(dkv_vm, dkv_hbm, out_sem.at[4])
     dkv_copy.start()
-    rd3(1)
-    rd3(2)
     rd3(last)
     gb_buf[my_b] = ga_finish()
     gb_start()
@@ -525,6 +547,7 @@
             pltpu.VMEM((T, 4096), BF),
             pltpu.VMEM((T, 4096), BF),
             pltpu.VMEM((T, 2, 512), BF),
+            pltpu.VMEM((KVH, T, 2, HD), BF),
             pltpu.VMEM((T, 2, 512), BF),
             pltpu.VMEM((T, 2, 512), BF),
             pltpu.VMEM((heads, HD, T), F32),
@@ -568,7 +591,7 @@
             dma((7,)),
             dma((6,)),
             dma((KVH,)),
-            dma((KVH,)),
+            dma((2 * KVH,)),
             dma((KVH, NX)),
             dma((KVH, NX)),
             dma((KVH,)),

time: 60 us -> 58 us (0.967)
  Pallas kernels: 57.3 us -> 55.3 us
    pallas_call x1, Pallas kernels: 54.5 us -> 52.4 us  [body(): pl.pallas_call(kernel, out_shape=shapes, in_specs=[anywhere] * 10, out_sp...]
where the time goes in v4:
time: 58 us; the launch traced here: 57.8 us
  Pallas kernels  55.3 us (95%)
  between operations  2.58 us (4%)
    pallas_call x1, Pallas kernels, body(): pl.pallas_call(kernel, out_shape=shapes, in_specs=[anywhere] * 10, out_sp...  52.4 us
    pallas_call x1, Pallas kernels, body(): pl.pallas_call(finish, out_shape=shapes, in_specs=[anywhere] * 4, out_spe...  2.82 us

profile of v4, /device:TPU:1, one launch (start us, length us, event | category | flops | bytes accessed | tf_op | source)
XLA Modules:
  0.0 57.8 jit_solution(8554962769835503532)
XLA Ops:
  2.6 52.4 %shard_map.129 = (bf16[256,4096]{1,0:T(8,128)(2,1)}, bf16[256,2,512]{2,1,0:T(2,128)(2,1)}, bf16[256,2,512]{2,1,0:T(2,128)(2,1)}, f32[2,128]{1,0:T(2,128)}) custom-call(bf16[256,4096]{1,0:T(8,128)(2,1)} %bitcast.7, bf16[256,2,512]{2,1,0:T(2,128)(2,1)} %bitcast.9, bf16[256,2,512]{2,1,0:T(2,128)(2,1)} %bitcast.10, f32[2,128]{1,0:T(2,128)} %gain_hbm.1, ...), custom_call_target="tpu_custom_call" | custom-call | tf_op jit(solution)/shard_map/pallas_call | solution.py:535
  55.0 2.8 %shard_map.130 = (bf16[256,4096]{1,0:T(8,128)(2,1)}, bf16[256,2,512]{2,1,0:T(2,128)(2,1)}, bf16[256,2,512]{2,1,0:T(2,128)(2,1)}, f32[2,128]{1,0:T(2,128)}) custom-call(bf16[256,4096]{1,0:T(8,128)(2,1)} %get-tuple-element.12.refs_0_, bf16[256,2,512]{2,1,0:T(2,128)(2,1)} %get-tuple-element.13.refs_1_, bf16[256,2,512]{2,1,0:T(2,128)(2,1)} %get-tuple-element.14.refs_2_, ...), custom_call_target="tpu_custom_call" | custom-call | tf_op jit(solution)/shard_map/pallas_call | solution.py:621

commit v5 on v4

--- a/solution.py
+++ b/solution.py
@@ -297,9 +297,12 @@
         for j in range(GW):
             first_part(g, j)
 
+        @pl.when(g == 1)
+        def _():
+            bc1(0)
+
         @pl.when(g == 2)
         def _():
-            bc1(0)
             bc1(1)
 
         @pl.when(g == 3)
@@ -476,12 +479,12 @@
 
     rd3(1)
     rd3(2)
+    rd3(last)
+    gb_buf[my_b] = ga_finish()
+    gb_start()
     lax.fori_loop(0, KVH, value_grads, 0)
     dkv_copy = pltpu.make_async_copy(dkv_vm, dkv_hbm, out_sem.at[4])
     dkv_copy.start()
-    rd3(last)
-    gb_buf[my_b] = ga_finish()
-    gb_start()
     rd4(0)
     rd4(1)
     rd4(2)

time: 58 us -> 58.3 us (level)
  no operation moved by 1% of the time
where the time goes in v5:
time: 58.3 us; the launch traced here: 58.2 us
  Pallas kernels  55.6 us (95%)
  between operations  2.58 us (4%)
    pallas_call x1, Pallas kernels, body(): pl.pallas_call(kernel, out_shape=shapes, in_specs=[anywhere] * 10, out_sp...  52.8 us
    pallas_call x1, Pallas kernels, body(): pl.pallas_call(finish, out_shape=shapes, in_specs=[anywhere] * 4, out_spe...  2.82 us

profile of v5, /device:TPU:1, one launch (start us, length us, event | category | flops | bytes accessed | tf_op | source)
XLA Modules:
  0.0 58.2 jit_solution(17754001910718374762)
XLA Ops:
  2.6 52.8 %shard_map.129 = (bf16[256,4096]{1,0:T(8,128)(2,1)}, bf16[256,2,512]{2,1,0:T(2,128)(2,1)}, bf16[256,2,512]{2,1,0:T(2,128)(2,1)}, f32[2,128]{1,0:T(2,128)}) custom-call(bf16[256,4096]{1,0:T(8,128)(2,1)} %bitcast.7, bf16[256,2,512]{2,1,0:T(2,128)(2,1)} %bitcast.9, bf16[256,2,512]{2,1,0:T(2,128)(2,1)} %bitcast.10, f32[2,128]{1,0:T(2,128)} %gain_hbm.1, ...), custom_call_target="tpu_custom_call" | custom-call | tf_op jit(solution)/shard_map/pallas_call | solution.py:538
  55.4 2.8 %shard_map.130 = (bf16[256,4096]{1,0:T(8,128)(2,1)}, bf16[256,2,512]{2,1,0:T(2,128)(2,1)}, bf16[256,2,512]{2,1,0:T(2,128)(2,1)}, f32[2,128]{1,0:T(2,128)}) custom-call(bf16[256,4096]{1,0:T(8,128)(2,1)} %get-tuple-element.12.refs_0_, bf16[256,2,512]{2,1,0:T(2,128)(2,1)} %get-tuple-element.13.refs_1_, bf16[256,2,512]{2,1,0:T(2,128)(2,1)} %get-tuple-element.14.refs_2_, ...), custom_call_target="tpu_custom_call" | custom-call | tf_op jit(solution)/shard_map/pallas_call | solution.py:624
